TPU v7x, 256 devices: a whole 4x4x8 slice. The times are simulated.
256 devices in a mesh: prompt: 8 (over z_hi, x), seq: 32 (over y, z_lo, core).
Axes of the slice: x: 4, y: 4, z: 8 (z_hi: 2, z_lo: 4; z = z_hi * 4 + z_lo), core: 2. Of those that a mesh axis runs over, the one named last changes fastest.
Arguments:
- queries: bfloat16 [8, 2, 1536, 8192], P('prompt', None, 'seq'), as said below
- resp_kv: bfloat16 [8, 2, 1536, 2048], P('prompt', None, 'seq'), as said below
- prompt_kv: bfloat16 [8, 1024, 2048], P(None, 'seq', 'prompt'), may hold values from -6 to 6
- block_order: int32 [8, 32], P('prompt'), may hold values from 0 to 31, each once within a row
- prompt_len: int32 [8], P('prompt'), may hold values from 256 to 1024, as said below
- resp_len: int32 [8, 2], P('prompt'), may hold values from 384 to 1536, as said below
Outputs:
- attended: bfloat16 [8, 2, 1536, 8192], P('prompt', None, 'seq')
Inputs may be any that keep to these rules, and one draw needn't show every extreme that they name: `prompt_len`: at least 256; one prompt has exactly 1024. `resp_len`: at least 384; one response has exactly 1536. `block_order`: each row names every storage block's prompt block once. `queries`: real values. `resp_kv`: real values.
All inputs are finite; a program needn't handle non-finite values.
Results may differ from a plain program's by a relative error of at most 0.008.
Values may be sent and summed in bfloat16 or wider, within the bound.
A program may use at most 128 MiB of HBM per device.

v0:
```python
import math

import jax
import jax.numpy as jnp
from jax import lax
from jax.sharding import PartitionSpec as P

H = 64
KVH = 8
HD = 128


def attend_block(carry, query, keys, values, mask, score_form, value_form):
    best, total, accum = carry
    scores = jnp.einsum(score_form, query, keys, preferred_element_type=jnp.float32) / math.sqrt(
        query.shape[-1]
    )
    scores = jnp.where(mask, scores, -1e30)
    new_best = jnp.maximum(best, jnp.max(scores, axis=-1))
    weights = jnp.where(mask, jnp.exp(scores - new_best[..., None]), 0.0)
    rescale = jnp.exp(best - new_best)
    total = total * rescale + jnp.sum(weights, axis=-1)
    accum = accum * rescale[..., None] + jnp.einsum(
        value_form, weights.astype(jnp.bfloat16), values, preferred_element_type=jnp.float32
    )
    return (new_best, total, accum)


def sweep_keys(carry, query, keyvals, key_axis, mask_of, score_form, value_form):
    count = keyvals.shape[key_axis]
    block = math.gcd(count, 512)
    head_dim = query.shape[-1]

    def advance(index, state):
        begin = index * block
        piece = lax.dynamic_slice_in_dim(keyvals, begin, block, key_axis)
        return attend_block(
            state,
            query,
            piece[..., :head_dim],
            piece[..., head_dim:],
            mask_of(begin, block),
            score_form,
            value_form,
        )

    return lax.fori_loop(0, count // block, advance, carry)


def prompt_mask(offset, count, block_order, prompt_len, block_rows, seq_count):
    index = offset + jnp.arange(count, dtype=jnp.int32)
    owner = index // block_rows
    match = owner[None, :, None] == jnp.arange(seq_count, dtype=jnp.int32)[None, None, :]
    logical = jnp.sum(jnp.where(match, block_order[:, None, :], 0), axis=2)
    position = logical * block_rows + index % block_rows
    valid = position < prompt_len[:, None]
    return valid[:, None, None, None, :]


def shards(queries, resp_kv, prompt_kv, block_order, prompt_len, resp_len):
    seq_count = lax.axis_size("seq")
    prompts_dev, cand_count, row_count, width = queries.shape
    heads_dev = H // seq_count
    slot_repeat = seq_count // KVH
    block_rows = prompt_kv.shape[1]
    full_rows = row_count * seq_count
    prompt_store = lax.all_to_all(prompt_kv, "prompt", split_axis=0, concat_axis=2, tiled=True)
    query_split = queries.reshape(prompts_dev, cand_count, row_count, seq_count, heads_dev * HD)
    query_heads = lax.all_to_all(query_split, "seq", split_axis=3, concat_axis=2, tiled=True)
    whole_kv = lax.all_gather(resp_kv, "seq", axis=2, tiled=True)
    head_start = lax.axis_index("seq") // slot_repeat * (2 * HD)
    kv_mine = lax.dynamic_slice_in_dim(whole_kv, head_start, 2 * HD, 3)
    query_mine = query_heads.reshape(prompts_dev, cand_count, full_rows, heads_dev, HD)
    lead_shape = (prompts_dev, cand_count, full_rows, heads_dev)
    initial = (
        jnp.full(lead_shape, -1e30, jnp.float32),
        jnp.zeros(lead_shape, jnp.float32),
        jnp.zeros(lead_shape + (HD,), jnp.float32),
    )
    head_offset = lax.axis_index("seq") // slot_repeat * (2 * HD)
    whole_prompt = lax.all_gather(prompt_store, "seq", axis=1, tiled=True)

    def mask_of(begin, count):
        return prompt_mask(0 + begin, count, block_order, prompt_len, block_rows, seq_count)

    carry = sweep_keys(
        initial,
        query_mine,
        lax.dynamic_slice_in_dim(whole_prompt, head_offset, 2 * HD, 2),
        1,
        mask_of,
        "pcrhd,pkd->pcrhk",
        "pcrhk,pkd->pcrhd",
    )
    query_pos = jnp.arange(full_rows, dtype=jnp.int32)

    def resp_mask(begin, count):
        key_pos = begin + jnp.arange(count, dtype=jnp.int32)
        causal = key_pos[None, None, None, None, :] <= query_pos[None, None, :, None, None]
        live = key_pos[None, None, None, None, :] < resp_len[:, :, None, None, None]
        return causal & live

    best, total, accum = sweep_keys(
        carry, query_mine, kv_mine, 2, resp_mask, "pcrhd,pckd->pcrhk", "pcrhk,pckd->pcrhd"
    )
    row_live = (query_pos[None, None, :] < resp_len[:, :, None]).astype(jnp.float32)
    result = (accum / total[..., None] * row_live[:, :, :, None, None]).astype(jnp.bfloat16)
    result = result.reshape(prompts_dev, cand_count, full_rows, 1, heads_dev * HD)
    back = lax.all_to_all(result, "seq", split_axis=2, concat_axis=3, tiled=True)
    return back.reshape(prompts_dev, cand_count, row_count, width)


def solution(mesh):
    in_specs = (
        P("prompt", None, "seq", None),
        P("prompt", None, "seq", None),
        P(None, "seq", "prompt"),
        P("prompt", None),
        P("prompt"),
        P("prompt", None),
    )
    out_specs = P("prompt", None, "seq", None)
    return jax.shard_map(shards, mesh=mesh, in_specs=in_specs, out_specs=out_specs, check_vma=False)
```

profile of v0, /device:TPU:25, one launch (start us, length us, event | category | flops | bytes accessed | tf_op | source)
XLA Modules:
  0.0 314.3 jit_solution(13371856088151074913)
XLA Ops:
  6.5 20.0 %all_to_all.48 = bf16[8,32,256]{2,1,0:T(8,128)(2,1)S(1)} all-to-all(bf16[8,32,256]{2,1,0:T(8,128)(2,1)} %param.12), channel_id=1, replica_groups=mesh['prompt'=8,'seq'=32] {'prompt'}, dimensions={0} | all-to-all | bytes 262144 | tf_op jit(solution)/shard_map/all_to_all | solution.py:67
  26.5 0.7 copy.66
  27.3 0.7 all-gather.5.cloned.1.call-update
  28.0 2.7 copy.68
  30.7 8.0 %all-to-all-start.1 = ((bf16[1,2,48,32,256]{4,2,1,0,3:T(8,128)(2,1)}), bf16[1,2,48,32,256]{4,2,1,0,3:T(8,128)(2,1)S(1)}, u32[]{:S(2)}, u32[]{:S(2)}) async-start(bf16[1,2,48,32,256]{4,2,1,0,3:T(8,128)(2,1)} %bitcast.123), calls=%async_computation.1 | async-start | bytes 3145728 | tf_op jit(solution)/shard_map/all_to_all | solution.py:69
  38.8 0.7 compare_convert_fusion
  39.5 51.6 %all-to-all-done.1 = bf16[1,2,48,32,256]{4,2,1,0,3:T(8,128)(2,1)S(1)} async-done(((bf16[1,2,48,32,256]{4,2,1,0,3:T(8,128)(2,1)}), bf16[1,2,48,32,256]{4,2,1,0,3:T(8,128)(2,1)S(1)}, u32[]{:S(2)}, u32[]{:S(2)}) %all-to-all-start.1) | async-done | bytes 1572896 | tf_op jit(solution)/shard_map/all_to_all | solution.py:69
  91.2 0.4 reshape.381
  91.9 11.4 %all-gather.3.cloned.1.call-done = bf16[1,1024,2048]{2,1,0:T(8,128)(2,1)} async-done(((bf16[1,32,2048]{2,1,0:T(8,128)(2,1)}), bf16[1,1024,2048]{2,1,0:T(8,128)(2,1)}) %all-gather.3.cloned.1.call-update) | async-done | bytes 4194320 | tf_op jit(solution)/shard_map/all_gather | solution.py:81
  103.3 1.1 constant_dynamic-slice_fusion.1
  104.4 41.1 %while.39 = (s32[]{:T(128)}, f32[1,2,1536,2]{2,3,1,0:T(2,128)S(1)}, f32[1,2,1536,2]{2,3,1,0:T(2,128)S(1)}, f32[1,2,1536,2,128]{4,2,3,1,0:T(8,128)}, s32[1,32]{1,...) while((s32[]{:T(128)}, f32[1,2,1536,2]{2,3,1,0:T(2,128)S(1)}, ...), condition=%wide.region_4.5_spmd.clone, body=%wide.region_0.4_spmd.clone.sunk | while | flops 1653967872 | bytes 96611192 | solution.py:47
  104.5 0.7 fusion.65
  105.2 5.6 %bitcast_reduce_fusion.2 = (f32[2,1536,2]{1,2,0:T(2,128)S(1)}, f32[512,2,1536,2]{2,0,3,1:T(8,128)}) fusion(pred[512]{0:T(512)(128)(4,1)S(1)} %fusion.65, bf16[1,2,1536,2,128]{4,2,3,1,0:T(8,128)(2,1)S(1)} %get-tuple-element.650, bf16[1,1024,256]{2,1,0:T(8,128)(2,1)S(1)} %get-tuple-element.649, s32[]{:T(128)S(6)} %select_n.225), kind=kOutput, calls=%fused_computation.28.clone.1 | convolution fusion | flops 814737408 | bytes 14311940 | tf_op jit(solution)/shard_map/while/body/eval_jaxpr/pcrhd,pkd->pcrhk/dot_general | solution.py:15
  110.9 8.7 %fusion.68 = f32[1,2,1536,2,128]{4,2,3,1,0:T(8,128)} fusion(f32[512,2,1536,2]{2,0,3,1:T(8,128)} %get-tuple-element.615, f32[2,1536,2]{1,2,0:T(2,128)S(1)} %bitcast.170, pred[512]{0:T(512)(128)(4,1)S(1)} %fusion.65, f32[1,2,1536,2,128]{4,2,3,1,0:T(8,128)} %get-tuple-element.633, f32[2,1536,2]{1,2,0:T(2,128)S(1)} %get-tuple-element.616, ...), kind=kOutput, calls=%fused_computation.38.clone.1 | convolution fusion | flops 823394304 | bytes 19055624 | tf_op jit(solution)/shard_map/while/body/eval_jaxpr/pcrhk,pkd->pcrhd/dot_general | solution.py:23
  119.6 0.9 copy-done
  120.5 3.7 %fusion.67 = f32[2,1536,2]{1,2,0:T(2,128)S(1)} fusion(f32[512,2,1536,2]{2,0,3,1:T(8,128)S(1)} %copy-done, f32[2,1536,2]{1,2,0:T(2,128)S(1)} %bitcast.171, pred[512]{0:T(512)(128)(4,1)S(1)} %fusion.65), kind=kLoop, calls=%fused_computation.33.clone.1 | loop fusion | flops 15722496 | bytes 12632576 | tf_op jit(solution)/shard_map/while/body/eval_jaxpr/reduce_sum | solution.py:22
  124.4 0.7 fusion.65
  125.1 5.8 %bitcast_reduce_fusion.2 = (f32[2,1536,2]{1,2,0:T(2,128)S(1)}, f32[512,2,1536,2]{2,0,3,1:T(8,128)}) fusion(pred[512]{0:T(512)(128)(4,1)S(1)} %fusion.65, bf16[1,2,1536,2,128]{4,2,3,1,0:T(8,128)(2,1)S(1)} %get-tuple-element.650, bf16[1,1024,256]{2,1,0:T(8,128)(2,1)S(1)} %get-tuple-element.649, s32[]{:T(128)S(6)} %select_n.225), kind=kOutput, calls=%fused_computation.28.clone.1 | convolution fusion | flops 814737408 | bytes 14311940 | tf_op jit(solution)/shard_map/while/body/eval_jaxpr/pcrhd,pkd->pcrhk/dot_general | solution.py:15
  131.0 9.4 %fusion.68 = f32[1,2,1536,2,128]{4,2,3,1,0:T(8,128)} fusion(f32[512,2,1536,2]{2,0,3,1:T(8,128)} %get-tuple-element.615, f32[2,1536,2]{1,2,0:T(2,128)S(1)} %bitcast.170, pred[512]{0:T(512)(128)(4,1)S(1)} %fusion.65, f32[1,2,1536,2,128]{4,2,3,1,0:T(8,128)} %get-tuple-element.633, f32[2,1536,2]{1,2,0:T(2,128)S(1)} %get-tuple-element.616, ...), kind=kOutput, calls=%fused_computation.38.clone.1 | convolution fusion | flops 823394304 | bytes 19055624 | tf_op jit(solution)/shard_map/while/body/eval_jaxpr/pcrhk,pkd->pcrhd/dot_general | solution.py:23
  140.4 1.4 copy-done
  141.7 3.7 %fusion.67 = f32[2,1536,2]{1,2,0:T(2,128)S(1)} fusion(f32[512,2,1536,2]{2,0,3,1:T(8,128)S(1)} %copy-done, f32[2,1536,2]{1,2,0:T(2,128)S(1)} %bitcast.171, pred[512]{0:T(512)(128)(4,1)S(1)} %fusion.65), kind=kLoop, calls=%fused_computation.33.clone.1 | loop fusion | flops 15722496 | bytes 12632576 | tf_op jit(solution)/shard_map/while/body/eval_jaxpr/reduce_sum | solution.py:22
  145.5 36.7 %all-gather.5.cloned.1.call-done = bf16[1,2,1536,2048]{3,2,1,0:T(8,128)(2,1)} async-done(((bf16[1,2,48,2048]{3,2,1,0:T(8,128)(2,1)}), bf16[1,2,1536,2048]{3,2,1,0:T(8,128)(2,1)}) %all-gather.5.cloned.1.call-update) | async-done | bytes 12582928 | tf_op jit(solution)/shard_map/all_gather | solution.py:70
  182.3 2.7 constant_dynamic-slice_fusion
  184.9 67.1 %while.38 = (s32[]{:T(128)}, f32[1,2,1536,2]{2,3,1,0:T(2,128)S(1)}, f32[1,2,1536,2]{2,3,1,0:T(2,128)S(1)}, f32[1,2,1536,2,128]{4,2,3,1,0:T(8,128)}, s32[1,2]{1,0...) while((s32[]{:T(128)}, f32[1,2,1536,2]{2,3,1,0:T(2,128)S(1)}, ...), condition=%wide.region_8.9_spmd.clone, body=%wide.region_5.8_spmd.clone.sunk | while | flops 1655459328 | bytes 104734944 | solution.py:47
  185.0 0.5 iota_compare_fusion.3
  185.5 0.9 broadcast_and_fusion.2
  186.4 7.1 %fusion.60 = (f32[2,1536,2]{1,2,0:T(2,128)S(1)}, f32[2,512,1536,2]{2,1,3,0:T(8,128)}) fusion(pred[2,1536,512]{1,2,0:T(8,128)(4,1)S(1)} %broadcast_and_fusion.2, bf16[1,2,1536,2,128]{4,2,3,1,0:T(8,128)(2,1)S(1)} %get-tuple-element.686, bf16[1,2,1536,256]{3,2,1,0:T(8,128)(2,1)} %get-tuple-element.685, s32[]{:T(128)S(6)} %select_n.216), kind=kOutput, calls=%fused_computation.3.clone.1 | convolution fusion | flops 814737408 | bytes 16015364 | tf_op jit(solution)/shard_map/while/body/eval_jaxpr/pcrhd,pckd->pcrhk/dot_general | solution.py:15
  193.6 9.2 %fusion.63 = f32[1,2,1536,2,128]{4,2,3,1,0:T(8,128)} fusion(f32[2,512,1536,2]{2,1,3,0:T(8,128)} %get-tuple-element.603, f32[2,1536,2]{1,2,0:T(2,128)S(1)} %bitcast.172, pred[2,1536,512]{1,2,0:T(8,128)(4,1)S(1)} %broadcast_and_fusion.2, f32[1,2,1536,2,128]{4,2,3,1,0:T(8,128)} %get-tuple-element.671, f32[2,1536,2]{1,2,0:T(2,128)S(1)} %get-tuple-element.604, ...), kind=kOutput, calls=%fused_computation.9.clone.1 | convolution fusion | flops 822607872 | bytes 20758536 | tf_op jit(solution)/shard_map/while/body/eval_jaxpr/pcrhk,pckd->pcrhd/dot_general | solution.py:23
  202.7 1.1 copy-done.1
  203.8 3.4 %fusion.62 = f32[2,1536,2]{1,2,0:T(2,128)S(1)} fusion(f32[2,512,1536,2]{2,1,3,0:T(8,128)S(1)} %copy-done.1, f32[2,1536,2]{1,2,0:T(2,128)S(1)} %bitcast.173, pred[2,1536,512]{1,2,0:T(8,128)(4,1)S(1)} %broadcast_and_fusion.2), kind=kLoop, calls=%fused_computation.5.clone.1 | loop fusion | flops 15722496 | bytes 14204928 | tf_op jit(solution)/shard_map/while/body/eval_jaxpr/reduce_sum | solution.py:22
  207.4 0.5 iota_compare_fusion.3
  207.9 0.9 broadcast_and_fusion.2
  208.8 7.1 %fusion.60 = (f32[2,1536,2]{1,2,0:T(2,128)S(1)}, f32[2,512,1536,2]{2,1,3,0:T(8,128)}) fusion(pred[2,1536,512]{1,2,0:T(8,128)(4,1)S(1)} %broadcast_and_fusion.2, bf16[1,2,1536,2,128]{4,2,3,1,0:T(8,128)(2,1)S(1)} %get-tuple-element.686, bf16[1,2,1536,256]{3,2,1,0:T(8,128)(2,1)} %get-tuple-element.685, s32[]{:T(128)S(6)} %select_n.216), kind=kOutput, calls=%fused_computation.3.clone.1 | convolution fusion | flops 814737408 | bytes 16015364 | tf_op jit(solution)/shard_map/while/body/eval_jaxpr/pcrhd,pckd->pcrhk/dot_general | solution.py:15
  215.9 9.2 %fusion.63 = f32[1,2,1536,2,128]{4,2,3,1,0:T(8,128)} fusion(f32[2,512,1536,2]{2,1,3,0:T(8,128)} %get-tuple-element.603, f32[2,1536,2]{1,2,0:T(2,128)S(1)} %bitcast.172, pred[2,1536,512]{1,2,0:T(8,128)(4,1)S(1)} %broadcast_and_fusion.2, f32[1,2,1536,2,128]{4,2,3,1,0:T(8,128)} %get-tuple-element.671, f32[2,1536,2]{1,2,0:T(2,128)S(1)} %get-tuple-element.604, ...), kind=kOutput, calls=%fused_computation.9.clone.1 | convolution fusion | flops 822607872 | bytes 20758536 | tf_op jit(solution)/shard_map/while/body/eval_jaxpr/pcrhk,pckd->pcrhd/dot_general | solution.py:23
  225.1 1.1 copy-done.1
  226.2 3.4 %fusion.62 = f32[2,1536,2]{1,2,0:T(2,128)S(1)} fusion(f32[2,512,1536,2]{2,1,3,0:T(8,128)S(1)} %copy-done.1, f32[2,1536,2]{1,2,0:T(2,128)S(1)} %bitcast.173, pred[2,1536,512]{1,2,0:T(8,128)(4,1)S(1)} %broadcast_and_fusion.2), kind=kLoop, calls=%fused_computation.5.clone.1 | loop fusion | flops 15722496 | bytes 14204928 | tf_op jit(solution)/shard_map/while/body/eval_jaxpr/reduce_sum | solution.py:22
  229.7 0.5 iota_compare_fusion.3
  230.2 0.9 broadcast_and_fusion.2
  231.2 7.1 %fusion.60 = (f32[2,1536,2]{1,2,0:T(2,128)S(1)}, f32[2,512,1536,2]{2,1,3,0:T(8,128)}) fusion(pred[2,1536,512]{1,2,0:T(8,128)(4,1)S(1)} %broadcast_and_fusion.2, bf16[1,2,1536,2,128]{4,2,3,1,0:T(8,128)(2,1)S(1)} %get-tuple-element.686, bf16[1,2,1536,256]{3,2,1,0:T(8,128)(2,1)} %get-tuple-element.685, s32[]{:T(128)S(6)} %select_n.216), kind=kOutput, calls=%fused_computation.3.clone.1 | convolution fusion | flops 814737408 | bytes 16015364 | tf_op jit(solution)/shard_map/while/body/eval_jaxpr/pcrhd,pckd->pcrhk/dot_general | solution.py:15
  238.3 9.2 %fusion.63 = f32[1,2,1536,2,128]{4,2,3,1,0:T(8,128)} fusion(f32[2,512,1536,2]{2,1,3,0:T(8,128)} %get-tuple-element.603, f32[2,1536,2]{1,2,0:T(2,128)S(1)} %bitcast.172, pred[2,1536,512]{1,2,0:T(8,128)(4,1)S(1)} %broadcast_and_fusion.2, f32[1,2,1536,2,128]{4,2,3,1,0:T(8,128)} %get-tuple-element.671, f32[2,1536,2]{1,2,0:T(2,128)S(1)} %get-tuple-element.604, ...), kind=kOutput, calls=%fused_computation.9.clone.1 | convolution fusion | flops 822607872 | bytes 20758536 | tf_op jit(solution)/shard_map/while/body/eval_jaxpr/pcrhk,pckd->pcrhd/dot_general | solution.py:23
  247.4 1.1 copy-done.1
  248.6 3.4 %fusion.62 = f32[2,1536,2]{1,2,0:T(2,128)S(1)} fusion(f32[2,512,1536,2]{2,1,3,0:T(8,128)S(1)} %copy-done.1, f32[2,1536,2]{1,2,0:T(2,128)S(1)} %bitcast.173, pred[2,1536,512]{1,2,0:T(8,128)(4,1)S(1)} %broadcast_and_fusion.2), kind=kLoop, calls=%fused_computation.5.clone.1 | loop fusion | flops 15722496 | bytes 14204928 | tf_op jit(solution)/shard_map/while/body/eval_jaxpr/reduce_sum | solution.py:22
  252.0 2.6 copy.55
  254.6 1.5 multiply_convert_fusion
  256.1 3.7 %copy.56 = bf16[1,2,1536,1,256]{4,1,3,0,2:T(2,128)(2,1)S(1)} copy(bf16[1,2,1536,1,256]{2,4,1,3,0:T(8,128)(2,1)} %bitcast.176) | data formatting | bytes 3145728 | tf_op jit(solution)/shard_map/reshape | solution.py:108
  259.8 44.9 %all_to_all.49 = bf16[1,2,1536,1,256]{4,1,3,0,2:T(2,128)(2,1)S(1)} all-to-all(bf16[1,2,1536,1,256]{4,1,3,0,2:T(2,128)(2,1)S(1)} %copy.56), channel_id=1, replica_groups=mesh['prompt'=8,'seq'=32] {'seq'}, dimensions={2} | all-to-all | bytes 3145728 | tf_op jit(solution)/shard_map/all_to_all | solution.py:109
  304.8 0.6 copy.58
  305.4 2.1 reshape.383
  (45 shorter events, 1.4 us)
Async XLA Ops:
  6.5 96.8 %all-gather.3.cloned.1.call-start = ((), (), s32[]{:S(2)}) async-start(), calls=%async_computation.3 | async-start | bytes 4325376 | tf_op jit(solution)/shard_map/all_gather | solution.py:81
  27.2 155.1 %all-gather.5.cloned.1.call-start = ((), (), s32[]{:S(2)}) async-start(), calls=%async_computation.4 | async-start | bytes 12976128 | tf_op jit(solution)/shard_map/all_gather | solution.py:70
  28.0 10.8 %copy-start.3 = (s32[1,2]{1,0:T(1,128)S(1)}, s32[1,2]{1,0:T(1,128)}, u32[]{:S(2)}) copy-start(s32[1,2]{1,0:T(1,128)} %param.15) | copy-start | bytes 28
  30.7 60.4 %all-to-all-start.1 = ((bf16[1,2,48,32,256]{4,2,1,0,3:T(8,128)(2,1)}), bf16[1,2,48,32,256]{4,2,1,0,3:T(8,128)(2,1)S(1)}, u32[]{:S(2)}, u32[]{:S(2)}) async-start(bf16[1,2,48,32,256]{4,2,1,0,3:T(8,128)(2,1)} %bitcast.123), calls=%async_computation.1 | async-start | bytes 3145728 | tf_op jit(solution)/shard_map/all_to_all | solution.py:69
  91.2 13.2 %copy-start.4 = (s32[1,32]{1,0:T(1,128)S(1)}, s32[1,32]{1,0:T(1,128)}, u32[]{:S(2)}) copy-start(s32[1,32]{1,0:T(1,128)} %param.13) | copy-start | bytes 388
  110.9 9.6 %copy-start = (f32[512,2,1536,2]{2,0,3,1:T(8,128)S(1)}, f32[512,2,1536,2]{2,0,3,1:T(8,128)}, u32[]{:S(2)}) copy-start(f32[512,2,1536,2]{2,0,3,1:T(8,128)} %get-tuple-element.615) | copy-start | bytes 37748740 | tf_op jit(solution)/shard_map/while
  131.0 10.8 %copy-start = (f32[512,2,1536,2]{2,0,3,1:T(8,128)S(1)}, f32[512,2,1536,2]{2,0,3,1:T(8,128)}, u32[]{:S(2)}) copy-start(f32[512,2,1536,2]{2,0,3,1:T(8,128)} %get-tuple-element.615) | copy-start | bytes 37748740 | tf_op jit(solution)/shard_map/while
  193.6 10.3 %copy-start.1 = (f32[2,512,1536,2]{2,1,3,0:T(8,128)S(1)}, f32[2,512,1536,2]{2,1,3,0:T(8,128)}, u32[]{:S(2)}) copy-start(f32[2,512,1536,2]{2,1,3,0:T(8,128)} %get-tuple-element.603) | copy-start | bytes 37748740 | tf_op jit(solution)/shard_map/while
  215.9 10.3 %copy-start.1 = (f32[2,512,1536,2]{2,1,3,0:T(8,128)S(1)}, f32[2,512,1536,2]{2,1,3,0:T(8,128)}, u32[]{:S(2)}) copy-start(f32[2,512,1536,2]{2,1,3,0:T(8,128)} %get-tuple-element.603) | copy-start | bytes 37748740 | tf_op jit(solution)/shard_map/while
  238.3 10.3 %copy-start.1 = (f32[2,512,1536,2]{2,1,3,0:T(8,128)S(1)}, f32[2,512,1536,2]{2,1,3,0:T(8,128)}, u32[]{:S(2)}) copy-start(f32[2,512,1536,2]{2,1,3,0:T(8,128)} %get-tuple-element.603) | copy-start | bytes 37748740 | tf_op jit(solution)/shard_map/while
  252.0 2.6 copy-start.2
Sparse Core Ops, SparseCore 0:
  27.3 75.9 all-gather.2
  105.1 77.1 all-gather.4
where the time goes:
time: 318 us; the launch traced here: 314 us
  waiting for transfers between devices  101 us (32%)
  matrix products  78.2 us (25%)
  blocking collectives  64.8 us (20%)
  other arithmetic  26.2 us (8%)
  local copies, waits for them, and re-layouts  22.6 us (7%)
  between operations  13.6 us (4%)
  starting transfers between devices  8.04 us (3%)
    all_to_all x1, waiting for transfers between devices, shards(): lax.all_to_all(query_split, 'seq', split_axis=3, concat_axis=2, tiled=True)  51.6 us
    dot_general x5, matrix products, attend_block(): jnp.einsum(value_form, weights.astype(jnp.bfloat16), values, preferred_el...  45.6 us
    all_to_all x1, blocking collectives, shards(): lax.all_to_all(result, 'seq', split_axis=2, concat_axis=3, tiled=True)  44.9 us
    all_gather x1, waiting for transfers between devices, shards(): whole_kv = lax.all_gather(resp_kv, 'seq', axis=2, tiled=True)  36.7 us
    dot_general x5, matrix products, attend_block(): jnp.einsum(score_form, query, keys, preferred_element_type=jnp.float32)  32.6 us
    all_to_all x1, blocking collectives, shards(): lax.all_to_all(prompt_kv, 'prompt', split_axis=0, concat_axis=2, tiled=True)  20 us
    reduce_sum x5, other arithmetic, attend_block(): total = total * rescale + jnp.sum(weights, axis=-1)  17.5 us
    all_gather x1, waiting for transfers between devices, shards(): whole_prompt = lax.all_gather(prompt_store, 'seq', axis=1, tiled=True)  11.4 us
  transfers between devices with their start and end apart: 3, of which 3 were waited for; matrix products, arithmetic and copies ran while one was open for 14% of the time, Pallas kernels for 0%

commit v1 on v0

v1 whole, which is shorter than its diff:
```python
import functools
import math

import jax
import jax.numpy as jnp
from jax import lax
from jax.experimental import pallas as pl
from jax.experimental.pallas import tpu as pltpu
from jax.sharding import PartitionSpec as P

H = 64
KVH = 8
HD = 128
CP = 32
NP = 8
NY, NZ, NC = 4, 4, 2
ROWS = 48
GROUP = H // KVH
QW = GROUP * HD
KVW = 2 * HD
SEG = NZ * NC * ROWS
RT = GROUP * NC * ROWS
PCH = 512
NPROMPT = NY * NZ * NC * CP
SCALE = math.log2(math.e) / math.sqrt(HD)
MESH = pl.DeviceIdType.MESH
NEG = -1e30


def kernel(
    q_in, r_in, p_in, order, plen, rlen, out,
    qbuf, rbuf, pbuf, obuf, kp, vp, sbuf, mbuf, accbuf, bias,
    q_s, q_r, r_s, r_r, p_s, p_r, zp_s, zp_r, zr_s, zr_r, o_s, o_r,
):
    p = lax.axis_index("prompt")
    s = lax.axis_index("seq")
    y = s // (NZ * NC)
    z = lax.rem(s, NZ * NC) // NC
    c = lax.rem(s, NC)
    mine = y * NC + c
    home = lax.div(p, NC) * (NZ * NC) + z * NC + lax.rem(p, NC)

    def seq_of(index, zz):
        return lax.div(index, NC) * (NZ * NC) + zz * NC + lax.rem(index, NC)

    def at_rel(k):
        return lax.rem(mine + k, NY * NC)

    def remote(src, dst, ss, rs, dev):
        return pltpu.make_async_remote_copy(
            src_ref=src, dst_ref=dst, send_sem=ss, recv_sem=rs, device_id=dev, device_id_type=MESH
        )

    def landed(ref, sem):
        pltpu.make_async_copy(ref, ref, sem).wait()

    barrier = pltpu.get_barrier_semaphore()

    def greet(dev):
        pl.semaphore_signal(barrier, inc=1, device_id=dev, device_id_type=MESH)

    for k in range(1, NY * NC):
        greet((p, seq_of(at_rel(k), z)))
    for k in range(1, NZ):
        greet((p, y * (NZ * NC) + lax.rem(z + k, NZ) * NC + c))
    for k in range(1, NP):
        greet((lax.rem(p + k, NP), home))
    for k in range(1, NY * NC):
        greet((mine, seq_of(at_rel(k), z)))

    @pl.when(p != mine)
    def _():
        greet((p, home))
        greet((mine, s))

    extra = jnp.where(p != mine, 2, 0)
    pl.semaphore_wait(barrier, (NY * NC - 1) * 2 + (NZ - 1) + (NP - 1) + extra)

    def r_copy(k):
        t = at_rel(k)
        src = r_in.at[0, :, :, pl.ds(pl.multiple_of(t * KVW, KVW), KVW)]
        dst = rbuf.at[:, y, z, c]
        if k == 0:
            return pltpu.make_async_copy(src, dst, r_r.at[mine])
        return remote(src, dst, r_s.at[k], r_r.at[mine], (p, seq_of(t, z)))

    def q_copy(k):
        t = at_rel(k)
        src = q_in.at[0, :, :, pl.ds(pl.multiple_of(t * QW, QW), QW)]
        dst = qbuf.at[y, c]
        if k == 0:
            return pltpu.make_async_copy(src, dst, q_r.at[mine])
        return remote(src, dst, q_s.at[k], q_r.at[mine], (p, seq_of(t, z)))

    def p_copy(k):
        t = lax.rem(p + k, NP)
        return remote(p_in.at[t], pbuf.at[y, z, c], p_s.at[k], p_r.at[mine], (t, home))

    def p_local():
        return pltpu.make_async_copy(p_in.at[p], pbuf.at[y, z, c], p_r.at[mine])

    for k in range(1, NP):
        p_copy(k).start()

    @pl.when(p != mine)
    def _():
        p_copy(0).start()

    @pl.when(p == mine)
    def _():
        p_local().start()

    for k in range(NY * NC):
        r_copy(k).start()
    for k in range(NY * NC):
        q_copy(k).start()

    def z_dev(zz):
        return (p, y * (NZ * NC) + zz * NC + c)

    def zp_copy(src_z, dst_z, slot):
        ref = pbuf.at[:, src_z]
        return remote(ref, ref, zp_s.at[slot], zp_r.at[src_z], z_dev(dst_z))

    def zr_copy(g, src_z, dst_z, slot):
        ref = rbuf.at[:, g, src_z]
        return remote(ref, ref, zr_s.at[g, slot], zr_r.at[g, src_z], z_dev(dst_z))

    def each_near(act):
        for slot, dz in enumerate((1, -1, 2, -2)):
            @pl.when(jnp.logical_and(z + dz >= 0, z + dz < NZ))
            def _(slot=slot, dz=dz):
                act(slot, z + dz)

    middle = jnp.logical_and(z > 0, z < NZ - 1)
    far_dst = (z - 1) * (NZ - 1)
    far_src = (NZ - 1) - far_dst

    for i in range(NY):
        for j in range(NC):
            landed(pbuf.at[i, z, j], p_r.at[i * NC + j])
    each_near(lambda slot, dz: zp_copy(z, dz, slot).start())
    for i in range(NY):
        for j in range(NC):
            landed(rbuf.at[:, i, z, j], r_r.at[i * NC + j])
        each_near(lambda slot, dz, i=i: zr_copy(i, z, dz, slot).start())

    @pl.when(middle)
    def _():
        landed(pbuf.at[:, far_src], zp_r.at[far_src])
        zp_copy(far_src, far_dst, 4).start()

    def relay_resp(i):
        @pl.when(middle)
        def _():
            landed(rbuf.at[:, i, far_src], zr_r.at[i, far_src])
            zr_copy(i, far_src, far_dst, 4).start()

    relay_resp(0)

    row_at = lax.broadcasted_iota(jnp.int32, (NC * ROWS, SEG), 0) + z * (NC * ROWS)
    col_at = lax.broadcasted_iota(jnp.int32, (NC * ROWS, SEG), 1)
    bias[...] = jnp.where(col_at <= row_at, 0.0, NEG)

    def wait_z(ref_of, sem_of):
        for k in range(1, NZ):
            src = lax.rem(z + k, NZ)
            relayed = jnp.logical_and(middle, src == far_src)

            @pl.when(jnp.logical_not(relayed))
            def _():
                landed(ref_of(src), sem_of(src))

    wait_z(lambda zz: pbuf.at[:, zz], lambda zz: zp_r.at[zz])

    positions = []
    for i in range(NY * NZ * NC):
        positions.append(order[0, i] * CP + lax.broadcasted_iota(jnp.int32, (CP, HD), 0))
    position = jnp.concatenate(positions, axis=0)
    live = position < plen[0]
    whole = pbuf[...].reshape(NPROMPT, KVW)
    keys = whole[:, :HD].astype(jnp.float32)
    vals = whole[:, HD:].astype(jnp.float32)
    first = jnp.sum(jnp.where(position == 0, keys, 0.0), axis=0, keepdims=True)
    kp[...] = jnp.where(live, keys, first).astype(jnp.bfloat16)
    vp[:, :HD] = jnp.where(live, vals, 0.0).astype(jnp.bfloat16)
    vp[:, HD:] = jnp.where(live, 1.0, 0.0).astype(jnp.bfloat16)

    dims = (((1,), (1,)), ((), ()))

    def lane_max(x):
        best = x[:, :HD]
        for t in range(1, x.shape[1] // HD):
            best = jnp.maximum(best, x[:, t * HD : (t + 1) * HD])
        return best

    def attend(g, cand):
        def q_rows():
            block = qbuf[g, :, cand]
            return jnp.concatenate(
                [block[:, :, h * HD : (h + 1) * HD].reshape(NC * ROWS, HD) for h in range(GROUP)], axis=0
            )

        mbuf[...] = jnp.full((RT, HD), NEG, jnp.float32)

        def score_prompt(t, _):
            at = pl.multiple_of(t * PCH, PCH)
            sc = lax.dot_general(q_rows(), kp[pl.ds(at, PCH), :], dims, preferred_element_type=jnp.float32)
            sbuf[:, pl.ds(at, PCH)] = sc
            mbuf[...] = jnp.maximum(mbuf[...], lane_max(sc))
            return 0

        lax.fori_loop(0, NPROMPT // PCH, score_prompt, 0)

        def resp_keys(t):
            return rbuf[cand, t].reshape(SEG, KVW)

        def score_resp(t, _):
            at = pl.multiple_of(NPROMPT + t * SEG, HD)
            sc = lax.dot_general(q_rows(), resp_keys(t)[:, :HD], dims, preferred_element_type=jnp.float32)
            sbuf[:, pl.ds(at, SEG)] = sc
            mbuf[...] = jnp.maximum(mbuf[...], lane_max(sc))
            return 0

        lax.fori_loop(0, g, score_resp, 0)
        at = pl.multiple_of(NPROMPT + g * SEG, HD)
        sc = lax.dot_general(q_rows(), resp_keys(g)[:, :HD], dims, preferred_element_type=jnp.float32)
        sc = (sc.reshape(GROUP, NC * ROWS, SEG) + bias[...][None]).reshape(RT, SEG)
        sbuf[:, pl.ds(at, SEG)] = sc
        best = jnp.max(jnp.maximum(mbuf[...], lane_max(sc)), axis=1, keepdims=True) * SCALE
        mbuf[...] = jnp.broadcast_to(best, (RT, HD))
        accbuf[...] = jnp.zeros((RT, KVW), jnp.float32)

        def weights(at, size):
            m = mbuf[...]
            m = jnp.concatenate([m] * (size // HD), axis=1)
            return jnp.exp2(sbuf[:, pl.ds(at, size)] * SCALE - m).astype(jnp.bfloat16)

        def add_prompt(t, _):
            at = pl.multiple_of(t * PCH, PCH)
            accbuf[...] += jnp.dot(weights(at, PCH), vp[pl.ds(at, PCH), :], preferred_element_type=jnp.float32)
            return 0

        lax.fori_loop(0, NPROMPT // PCH, add_prompt, 0)

        def add_resp(t, _):
            at = pl.multiple_of(NPROMPT + t * SEG, HD)
            vx = jnp.concatenate([resp_keys(t)[:, HD:], jnp.ones((SEG, HD), jnp.bfloat16)], axis=1)
            accbuf[...] += jnp.dot(weights(at, SEG), vx, preferred_element_type=jnp.float32)
            return 0

        lax.fori_loop(0, g + 1, add_resp, 0)
        acc = accbuf[...]
        res = (acc[:, :HD] / acc[:, HD:]).reshape(GROUP, NC * ROWS, HD)
        pos = lax.broadcasted_iota(jnp.int32, (NC * ROWS, HD), 0) + (g * SEG + z * (NC * ROWS))
        alive = pos < rlen[0, cand]
        for h in range(GROUP):
            piece = jnp.where(alive, res[h], 0.0).astype(jnp.bfloat16)
            obuf[g, :, cand, :, h * HD : (h + 1) * HD] = piece.reshape(NC, ROWS, HD)

    out_ref = out.at[0, :, :, pl.ds(pl.multiple_of(mine * QW, QW), QW)]

    def o_remote(g, j):
        return remote(obuf.at[g, j], out_ref, o_s.at[g, j], o_r.at[mine], (p, seq_of(g * NC + j, z)))

    def o_local(g, j):
        return pltpu.make_async_copy(obuf.at[g, j], out_ref, o_r.at[mine])

    def group_step(g, _):
        for j in range(NC):
            landed(qbuf.at[g, j], q_r.at[g * NC + j])
        wait_z(lambda zz: rbuf.at[:, g, zz], lambda zz: zr_r.at[g, zz])

        attend(g, 0)

        @pl.when(g < NY - 1)
        def _():
            relay_resp(g + 1)

        attend(g, 1)

        for j in range(NC):
            @pl.when(g * NC + j == mine)
            def _():
                o_local(g, j).start()

            @pl.when(g * NC + j != mine)
            def _():
                o_remote(g, j).start()
        return 0

    lax.fori_loop(0, NY, group_step, 0)

    for k in range(1, NY * NC):
        q_copy(k).wait_send()
        r_copy(k).wait_send()
        p_copy(k).wait_send()

    @pl.when(p != mine)
    def _():
        p_copy(0).wait_send()

    each_near(lambda slot, dz: zp_copy(z, dz, slot).wait_send())
    for i in range(NY):
        each_near(lambda slot, dz, i=i: zr_copy(i, z, dz, slot).wait_send())

    @pl.when(middle)
    def _():
        zp_copy(far_src, far_dst, 4).wait_send()
        for i in range(NY):
            zr_copy(i, far_src, far_dst, 4).wait_send()

    for i in range(NY):
        for j in range(NC):
            @pl.when(i * NC + j != mine)
            def _(i=i, j=j):
                o_remote(i, j).wait_send()

    for k in range(NY * NC):
        landed(out.at[0, :, :, pl.ds(k * QW, QW)], o_r.at[k])


def shards(queries, resp_kv, prompt_kv, block_order, prompt_len, resp_len):
    bf16, f32 = jnp.bfloat16, jnp.float32
    dma = pltpu.SemaphoreType.DMA
    any_spec = pl.BlockSpec(memory_space=pl.ANY)
    smem = pl.BlockSpec(memory_space=pltpu.SMEM)
    return pl.pallas_call(
        kernel,
        out_shape=jax.ShapeDtypeStruct(queries.shape, bf16),
        in_specs=[any_spec] * 3 + [smem] * 3,
        out_specs=any_spec,
        scratch_shapes=[
            pltpu.VMEM((NY, NC, 2, ROWS, QW), bf16),
            pltpu.VMEM((2, NY, NZ, NC, ROWS, KVW), bf16),
            pltpu.VMEM((NY, NZ, NC, CP, KVW), bf16),
            pltpu.VMEM((NY, NC, 2, ROWS, QW), bf16),
            pltpu.VMEM((NPROMPT, HD), bf16),
            pltpu.VMEM((NPROMPT, KVW), bf16),
            pltpu.VMEM((RT, NPROMPT + NY * SEG), f32),
            pltpu.VMEM((RT, HD), f32),
            pltpu.VMEM((RT, KVW), f32),
            pltpu.VMEM((NC * ROWS, SEG), f32),
            dma((NY * NC,)), dma((NY * NC,)),
            dma((NY * NC,)), dma((NY * NC,)),
            dma((NP,)), dma((NY * NC,)),
            dma((5,)), dma((NZ,)),
            dma((NY, 5)), dma((NY, NZ)),
            dma((NY, NC)), dma((NY * NC,)),
        ],
        compiler_params=pltpu.CompilerParams(
            collective_id=0, has_side_effects=True, vmem_limit_bytes=48 * 1024 * 1024
        ),
        name="attend",
    )(queries, resp_kv, prompt_kv, block_order, prompt_len, resp_len)


def solution(mesh):
    in_specs = (
        P("prompt", None, "seq", None),
        P("prompt", None, "seq", None),
        P(None, "seq", "prompt"),
        P("prompt", None),
        P("prompt"),
        P("prompt", None),
    )
    out_specs = P("prompt", None, "seq", None)
    return jax.shard_map(shards, mesh=mesh, in_specs=in_specs, out_specs=out_specs, check_vma=False)
```

time: 318 us -> 90.7 us (0.29); the launches traced: 314 us -> 90.5 us
  waiting for transfers between devices: 101 us -> 0 us
  Pallas kernels: 0 us -> 84 us
  matrix products: 78.2 us -> 0 us
  blocking collectives: 64.8 us -> 0 us
  other arithmetic: 26.2 us -> 0 us
  local copies, waits for them, and re-layouts: 22.6 us -> 5.75 us
  between operations: 13.6 us -> 0.67 us
  starting transfers between devices: 8.04 us -> 0 us
    pallas_call x0 -> x1, Pallas kernels: none -> 84 us  [shards(): pl.pallas_call(kernel, out_shape=jax.ShapeDtypeStruct(queries.shape, bf16...]
    dot_general x10 -> x0, matrix products: 78.2 us -> none  [the longest x5 45.6 us: attend_block(): jnp.einsum(value_form, weights.astype(jnp.bfloat16), values, preferred_el...]
    all_to_all x2 -> x0, blocking collectives: 64.8 us -> none  [the longest x1 44.9 us: shards(): lax.all_to_all(result, 'seq', split_axis=2, concat_axis=3, tiled=True)]
    all_to_all x1 -> x0, waiting for transfers between devices: 51.6 us -> none  [shards(): lax.all_to_all(query_split, 'seq', split_axis=3, concat_axis=2, tiled=True)]
    all_gather x2 -> x0, waiting for transfers between devices: 48.2 us -> none  [the longest x1 36.7 us: shards(): whole_kv = lax.all_gather(resp_kv, 'seq', axis=2, tiled=True)]
    reduce_sum x7 -> x0, other arithmetic: 17.7 us -> none  [the longest x5 17.5 us: attend_block(): total = total * rescale + jnp.sum(weights, axis=-1)]
    reshape x4 -> x0, local copies, waits for them, and re-layouts: 8.93 us -> none  [the longest x1 3.66 us: shards(): result.reshape(prompts_dev, cand_count, full_rows, 1, heads_dev * HD)]
    while x16 -> x0, local copies, waits for them, and re-layouts: 8.19 us -> none
  transfers between devices with their start and end apart: 3 -> 0, of which waited for: 3 -> 0; matrix products, arithmetic and copies ran while one was open for 14% -> 0% of each run, Pallas kernels for 0% -> 0%
where the time goes in v1:
time: 90.7 us; the launch traced here: 90.5 us
  Pallas kernels  84 us (93%)
  local copies, waits for them, and re-layouts  5.75 us (6%)
    pallas_call x1, Pallas kernels, shards(): pl.pallas_call(kernel, out_shape=jax.ShapeDtypeStruct(queries.shape, bf16...  84 us
    unnamed x11, local copies, waits for them, and re-layouts  5.75 us

profile of v1, /device:TPU:25, one launch (start us, length us, event | category | flops | bytes accessed | tf_op | source)
XLA Modules:
  0.0 90.5 jit_solution(9249181341313906892)
XLA Ops:
  0.7 0.0 copy-start
  0.7 1.4 %copy-done = bf16[1,2,48,8192]{3,2,1,0:T(8,128)(2,1)S(1)} copy-done((bf16[1,2,48,8192]{3,2,1,0:T(8,128)(2,1)S(1)}, bf16[1,2,48,8192]{3,2,1,0:T(8,128)(2,1)}, u32[]{:S(2)}) %copy-start) | copy-done | bytes 1572888
  2.1 0.0 copy-start.1
  2.1 1.0 %copy-done.1 = bf16[1,2,48,2048]{3,2,1,0:T(8,128)(2,1)S(1)} copy-done((bf16[1,2,48,2048]{3,2,1,0:T(8,128)(2,1)S(1)}, bf16[1,2,48,2048]{3,2,1,0:T(8,128)(2,1)}, u32[]{:S(2)}) %copy-start.1) | copy-done | bytes 393240
  3.1 0.0 copy-start.2
  3.1 0.9 copy-done.2
  4.0 0.0 copy-start.3
  4.0 0.7 copy-done.3
  4.6 0.0 copy-start.4
  4.6 0.7 copy-done.4
  5.3 84.0 %attend.1 = bf16[1,2,48,8192]{3,2,1,0:T(8,128)(2,1)S(1)} custom-call(bf16[1,2,48,8192]{3,2,1,0:T(8,128)(2,1)S(1)} %copy-done, bf16[1,2,48,2048]{3,2,1,0:T(8,128)(2,1)S(1)} %copy-done.1, bf16[8,32,256]{2,1,0:T(8,128)(2,1)S(1)} %copy-done.2, s32[1,32]{1,0:T(1,128)S(1)} %copy-done.3, s32[1]{0:T(128)S(6)} %copy.8.plen, s32[1,2]{1,0:T(1,128)S(1)} %copy-done.4), custom_call_target="tpu_custom_call" | custom-call | tf_op jit(solution)/shard_map/attend/pallas_call | solution.py:328
  89.3 1.1 %copy.9 = bf16[1,2,48,8192]{3,2,1,0:T(8,128)(2,1)} copy(bf16[1,2,48,8192]{3,2,1,0:T(8,128)(2,1)S(1)} %attend.1) | data formatting | bytes 3145728
Async XLA Ops:
  0.7 1.4 %copy-start = (bf16[1,2,48,8192]{3,2,1,0:T(8,128)(2,1)S(1)}, bf16[1,2,48,8192]{3,2,1,0:T(8,128)(2,1)}, u32[]{:S(2)}) copy-start(bf16[1,2,48,8192]{3,2,1,0:T(8,128)(2,1)} %q_in.1) | copy-start | bytes 4718596
  2.1 1.0 %copy-start.1 = (bf16[1,2,48,2048]{3,2,1,0:T(8,128)(2,1)S(1)}, bf16[1,2,48,2048]{3,2,1,0:T(8,128)(2,1)}, u32[]{:S(2)}) copy-start(bf16[1,2,48,2048]{3,2,1,0:T(8,128)(2,1)} %r_in.1) | copy-start | bytes 1179652
  3.1 0.9 copy-start.2
  4.0 0.7 copy-start.3
  4.6 0.7 copy-start.4

commit v2 on v1

--- a/solution.py
+++ b/solution.py
@@ -25,6 +25,8 @@
 SCALE = math.log2(math.e) / math.sqrt(HD)
 MESH = pl.DeviceIdType.MESH
 NEG = -1e30
+UNITS = 2 * NY
+AHEAD = 2
 
 
 def kernel(
@@ -84,13 +86,13 @@
             return pltpu.make_async_copy(src, dst, r_r.at[mine])
         return remote(src, dst, r_s.at[k], r_r.at[mine], (p, seq_of(t, z)))
 
-    def q_copy(k):
+    def q_copy(k, cand):
         t = at_rel(k)
-        src = q_in.at[0, :, :, pl.ds(pl.multiple_of(t * QW, QW), QW)]
-        dst = qbuf.at[y, c]
+        src = q_in.at[0, cand, :, pl.ds(pl.multiple_of(t * QW, QW), QW)]
+        dst = qbuf.at[cand, y, c]
         if k == 0:
-            return pltpu.make_async_copy(src, dst, q_r.at[mine])
-        return remote(src, dst, q_s.at[k], q_r.at[mine], (p, seq_of(t, z)))
+            return pltpu.make_async_copy(src, dst, q_r.at[cand, mine])
+        return remote(src, dst, q_s.at[cand, k], q_r.at[cand, mine], (p, seq_of(t, z)))
 
     def p_copy(k):
         t = lax.rem(p + k, NP)
@@ -112,8 +114,9 @@
 
     for k in range(NY * NC):
         r_copy(k).start()
-    for k in range(NY * NC):
-        q_copy(k).start()
+    for cand in range(2):
+        for k in range(NY * NC):
+            q_copy(k, cand).start()
 
     def z_dev(zz):
         return (p, y * (NZ * NC) + zz * NC + c)
@@ -122,39 +125,55 @@
         ref = pbuf.at[:, src_z]
         return remote(ref, ref, zp_s.at[slot], zp_r.at[src_z], z_dev(dst_z))
 
-    def zr_copy(g, src_z, dst_z, slot):
-        ref = rbuf.at[:, g, src_z]
-        return remote(ref, ref, zr_s.at[g, slot], zr_r.at[g, src_z], z_dev(dst_z))
-
-    def each_near(act):
-        for slot, dz in enumerate((1, -1, 2, -2)):
-            @pl.when(jnp.logical_and(z + dz >= 0, z + dz < NZ))
-            def _(slot=slot, dz=dz):
-                act(slot, z + dz)
+    def zr_copy(u, src_z, dst_z, slot):
+        ref = rbuf.at[u // NY, u % NY, src_z]
+        return remote(ref, ref, zr_s.at[u, slot], zr_r.at[u, src_z], z_dev(dst_z))
 
     middle = jnp.logical_and(z > 0, z < NZ - 1)
     far_dst = (z - 1) * (NZ - 1)
     far_src = (NZ - 1) - far_dst
 
+    def each_near(act, early, late):
+        for slot, dz in enumerate((1, -1, 2, -2)):
+            there = jnp.logical_and(z + dz >= 0, z + dz < NZ)
+            held = jnp.logical_and(middle, z + dz == far_dst)
+            want = there
+            if not early:
+                want = jnp.logical_and(there, held)
+            if not late:
+                want = jnp.logical_and(there, jnp.logical_not(held))
+
+            @pl.when(want)
+            def _(slot=slot, dz=dz):
+                act(slot, z + dz)
+
+    def send_unit(u, early, late):
+        each_near(lambda slot, dz: zr_copy(u, z, dz, slot).start(), early, late)
+
     for i in range(NY):
         for j in range(NC):
             landed(pbuf.at[i, z, j], p_r.at[i * NC + j])
-    each_near(lambda slot, dz: zp_copy(z, dz, slot).start())
+    each_near(lambda slot, dz: zp_copy(z, dz, slot).start(), True, True)
     for i in range(NY):
         for j in range(NC):
             landed(rbuf.at[:, i, z, j], r_r.at[i * NC + j])
-        each_near(lambda slot, dz, i=i: zr_copy(i, z, dz, slot).start())
+    for u in range(UNITS):
+        send_unit(u, True, u < AHEAD)
+
+    def relay_resp(u):
+        @pl.when(middle)
+        def _():
+            landed(rbuf.at[u // NY, u % NY, far_src], zr_r.at[u, far_src])
+            zr_copy(u, far_src, far_dst, 4).start()
+
+        @pl.when(u + AHEAD < UNITS)
+        def _():
+            send_unit(u + AHEAD, False, True)
 
     @pl.when(middle)
     def _():
         landed(pbuf.at[:, far_src], zp_r.at[far_src])
         zp_copy(far_src, far_dst, 4).start()
-
-    def relay_resp(i):
-        @pl.when(middle)
-        def _():
-            landed(rbuf.at[:, i, far_src], zr_r.at[i, far_src])
-            zr_copy(i, far_src, far_dst, 4).start()
 
     relay_resp(0)
 
@@ -194,9 +213,11 @@
             best = jnp.maximum(best, x[:, t * HD : (t + 1) * HD])
         return best
 
-    def attend(g, cand):
+    def attend(u):
+        cand, g = u // NY, lax.rem(u, NY)
+
         def q_rows():
-            block = qbuf[g, :, cand]
+            block = qbuf[cand, g]
             return jnp.concatenate(
                 [block[:, :, h * HD : (h + 1) * HD].reshape(NC * ROWS, HD) for h in range(GROUP)], axis=0
             )
@@ -231,6 +252,10 @@
         mbuf[...] = jnp.broadcast_to(best, (RT, HD))
         accbuf[...] = jnp.zeros((RT, KVW), jnp.float32)
 
+        @pl.when(u < UNITS - 1)
+        def _():
+            relay_resp(u + 1)
+
         def weights(at, size):
             m = mbuf[...]
             m = jnp.concatenate([m] * (size // HD), axis=1)
@@ -256,43 +281,43 @@
         alive = pos < rlen[0, cand]
         for h in range(GROUP):
             piece = jnp.where(alive, res[h], 0.0).astype(jnp.bfloat16)
-            obuf[g, :, cand, :, h * HD : (h + 1) * HD] = piece.reshape(NC, ROWS, HD)
-
-    out_ref = out.at[0, :, :, pl.ds(pl.multiple_of(mine * QW, QW), QW)]
-
-    def o_remote(g, j):
-        return remote(obuf.at[g, j], out_ref, o_s.at[g, j], o_r.at[mine], (p, seq_of(g * NC + j, z)))
-
-    def o_local(g, j):
-        return pltpu.make_async_copy(obuf.at[g, j], out_ref, o_r.at[mine])
-
-    def group_step(g, _):
-        for j in range(NC):
-            landed(qbuf.at[g, j], q_r.at[g * NC + j])
-        wait_z(lambda zz: rbuf.at[:, g, zz], lambda zz: zr_r.at[g, zz])
-
-        attend(g, 0)
-
-        @pl.when(g < NY - 1)
-        def _():
-            relay_resp(g + 1)
-
-        attend(g, 1)
-
+            obuf[cand, g, :, :, h * HD : (h + 1) * HD] = piece.reshape(NC, ROWS, HD)
+
+    def o_ref(cand, index):
+        return out.at[0, cand, :, pl.ds(pl.multiple_of(index * QW, QW), QW)]
+
+    def o_remote(u, j):
+        cand, g = u // NY, lax.rem(u, NY)
+        return remote(
+            obuf.at[cand, g, j], o_ref(cand, mine), o_s.at[u, j], o_r.at[cand, mine],
+            (p, seq_of(g * NC + j, z)),
+        )
+
+    def o_local(u, j):
+        cand, g = u // NY, lax.rem(u, NY)
+        return pltpu.make_async_copy(obuf.at[cand, g, j], o_ref(cand, mine), o_r.at[cand, mine])
+
+    def unit_step(u, _):
+        cand, g = u // NY, lax.rem(u, NY)
+        for j in range(NC):
+            landed(qbuf.at[cand, g, j], q_r.at[cand, g * NC + j])
+        wait_z(lambda zz: rbuf.at[cand, g, zz], lambda zz: zr_r.at[u, zz])
+        attend(u)
         for j in range(NC):
             @pl.when(g * NC + j == mine)
             def _():
-                o_local(g, j).start()
+                o_local(u, j).start()
 
             @pl.when(g * NC + j != mine)
             def _():
-                o_remote(g, j).start()
+                o_remote(u, j).start()
         return 0
 
-    lax.fori_loop(0, NY, group_step, 0)
+    lax.fori_loop(0, UNITS, unit_step, 0)
 
     for k in range(1, NY * NC):
-        q_copy(k).wait_send()
+        for cand in range(2):
+            q_copy(k, cand).wait_send()
         r_copy(k).wait_send()
         p_copy(k).wait_send()
 
@@ -300,24 +325,30 @@
     def _():
         p_copy(0).wait_send()
 
-    each_near(lambda slot, dz: zp_copy(z, dz, slot).wait_send())
-    for i in range(NY):
-        each_near(lambda slot, dz, i=i: zr_copy(i, z, dz, slot).wait_send())
+    each_near(lambda slot, dz: zp_copy(z, dz, slot).wait_send(), True, True)
 
     @pl.when(middle)
     def _():
         zp_copy(far_src, far_dst, 4).wait_send()
-        for i in range(NY):
-            zr_copy(i, far_src, far_dst, 4).wait_send()
-
-    for i in range(NY):
-        for j in range(NC):
-            @pl.when(i * NC + j != mine)
-            def _(i=i, j=j):
-                o_remote(i, j).wait_send()
-
-    for k in range(NY * NC):
-        landed(out.at[0, :, :, pl.ds(k * QW, QW)], o_r.at[k])
+
+    def end_step(u, _):
+        each_near(lambda slot, dz: zr_copy(u, z, dz, slot).wait_send(), True, True)
+
+        @pl.when(middle)
+        def _():
+            zr_copy(u, far_src, far_dst, 4).wait_send()
+
+        for j in range(NC):
+            @pl.when(lax.rem(u, NY) * NC + j != mine)
+            def _():
+                o_remote(u, j).wait_send()
+        return 0
+
+    lax.fori_loop(0, UNITS, end_step, 0)
+
+    for cand in range(2):
+        for k in range(NY * NC):
+            landed(o_ref(cand, k), o_r.at[cand, k])
 
 
 def shards(queries, resp_kv, prompt_kv, block_order, prompt_len, resp_len):
@@ -331,25 +362,25 @@
         in_specs=[any_spec] * 3 + [smem] * 3,
         out_specs=any_spec,
         scratch_shapes=[
-            pltpu.VMEM((NY, NC, 2, ROWS, QW), bf16),
+            pltpu.VMEM((2, NY, NC, ROWS, QW), bf16),
             pltpu.VMEM((2, NY, NZ, NC, ROWS, KVW), bf16),
             pltpu.VMEM((NY, NZ, NC, CP, KVW), bf16),
-            pltpu.VMEM((NY, NC, 2, ROWS, QW), bf16),
+            pltpu.VMEM((2, NY, NC, ROWS, QW), bf16),
             pltpu.VMEM((NPROMPT, HD), bf16),
             pltpu.VMEM((NPROMPT, KVW), bf16),
             pltpu.VMEM((RT, NPROMPT + NY * SEG), f32),
             pltpu.VMEM((RT, HD), f32),
             pltpu.VMEM((RT, KVW), f32),
             pltpu.VMEM((NC * ROWS, SEG), f32),
-            dma((NY * NC,)), dma((NY * NC,)),
+            dma((2, NY * NC)), dma((2, NY * NC)),
             dma((NY * NC,)), dma((NY * NC,)),
             dma((NP,)), dma((NY * NC,)),
             dma((5,)), dma((NZ,)),
-            dma((NY, 5)), dma((NY, NZ)),
-            dma((NY, NC)), dma((NY * NC,)),
+            dma((UNITS, 5)), dma((UNITS, NZ)),
+            dma((UNITS, NC)), dma((2, NY * NC)),
         ],
         compiler_params=pltpu.CompilerParams(
-            collective_id=0, has_side_effects=True, vmem_limit_bytes=48 * 1024 * 1024
+            collective_id=0, has_side_effects=True, vmem_limit_bytes=62 * 1024 * 1024
         ),
         name="attend",
     )(queries, resp_kv, prompt_kv, block_order, prompt_len, resp_len)

time: 90.7 us -> 78.1 us (0.86)
  Pallas kernels: 84 us -> 74.6 us
  local copies, waits for them, and re-layouts: 5.75 us -> 2.65 us
    pallas_call x1, Pallas kernels: 84 us -> 74.6 us  [shards(): pl.pallas_call(kernel, out_shape=jax.ShapeDtypeStruct(queries.shape, bf16...]
    unnamed x11 -> x1, local copies, waits for them, and re-layouts: 5.75 us -> 2.65 us
where the time goes in v2:
time: 78.1 us; the launch traced here: 77.9 us
  Pallas kernels  74.6 us (96%)
  local copies, waits for them, and re-layouts  2.65 us (3%)
    pallas_call x1, Pallas kernels, shards(): pl.pallas_call(kernel, out_shape=jax.ShapeDtypeStruct(queries.shape, bf16...  74.6 us
    unnamed x1, local copies, waits for them, and re-layouts  2.65 us

profile of v2, /device:TPU:25, one launch (start us, length us, event | category | flops | bytes accessed | tf_op | source)
XLA Modules:
  0.0 77.9 jit_solution(9607049325898028857)
XLA Ops:
  0.7 74.6 %attend.1 = bf16[1,2,48,8192]{3,2,1,0:T(8,128)(2,1)} custom-call(bf16[1,2,48,8192]{3,2,1,0:T(8,128)(2,1)} %q_in.1, bf16[1,2,48,2048]{3,2,1,0:T(8,128)(2,1)} %r_in.1, bf16[8,32,256]{2,1,0:T(8,128)(2,1)} %p_in.1, s32[1,32]{1,0:T(1,128)} %order.1, s32[1]{0:T(128)S(6)} %copy.8.plen, s32[1,2]{1,0:T(1,128)} %rlen.1), custom_call_target="tpu_custom_call" | custom-call | tf_op jit(solution)/shard_map/attend/pallas_call | solution.py:359
  75.2 2.7 %copy.9 = bf16[1,2,48,8192]{3,2,1,0:T(8,128)(2,1)} copy(bf16[1,2,48,8192]{3,2,1,0:T(8,128)(2,1)} %attend.1) | data formatting | bytes 3145728

commit v3 on v2

--- a/solution.py
+++ b/solution.py
@@ -20,12 +20,15 @@
 KVW = 2 * HD
 SEG = NZ * NC * ROWS
 RT = GROUP * NC * ROWS
-PCH = 512
 NPROMPT = NY * NZ * NC * CP
 SCALE = math.log2(math.e) / math.sqrt(HD)
 MESH = pl.DeviceIdType.MESH
 NEG = -1e30
 UNITS = 2 * NY
+TILE = 4
+TILES = GROUP // TILE
+TW = TILE * HD
+TR = TILE * NC * ROWS
 AHEAD = 2
 
 
@@ -101,6 +104,12 @@
     def p_local():
         return pltpu.make_async_copy(p_in.at[p], pbuf.at[y, z, c], p_r.at[mine])
 
+    r_copy(0).start()
+    for k in (1, NY * NC - 1):
+        @pl.when(at_rel(k) // NC == y)
+        def _(k=k):
+            r_copy(k).start()
+
     for k in range(1, NP):
         p_copy(k).start()
 
@@ -112,11 +121,10 @@
     def _():
         p_local().start()
 
-    for k in range(NY * NC):
-        r_copy(k).start()
-    for cand in range(2):
-        for k in range(NY * NC):
-            q_copy(k, cand).start()
+    for k in range(1, NY * NC):
+        @pl.when(at_rel(k) // NC != y)
+        def _(k=k):
+            r_copy(k).start()
 
     def z_dev(zz):
         return (p, y * (NZ * NC) + zz * NC + c)
@@ -126,7 +134,7 @@
         return remote(ref, ref, zp_s.at[slot], zp_r.at[src_z], z_dev(dst_z))
 
     def zr_copy(u, src_z, dst_z, slot):
-        ref = rbuf.at[u // NY, u % NY, src_z]
+        ref = rbuf.at[u // NY, lax.rem(u, NY), src_z]
         return remote(ref, ref, zr_s.at[u, slot], zr_r.at[u, src_z], z_dev(dst_z))
 
     middle = jnp.logical_and(z > 0, z < NZ - 1)
@@ -134,7 +142,7 @@
     far_src = (NZ - 1) - far_dst
 
     def each_near(act, early, late):
-        for slot, dz in enumerate((1, -1, 2, -2)):
+        for slot, dz in enumerate((2, -2, 1, -1)):
             there = jnp.logical_and(z + dz >= 0, z + dz < NZ)
             held = jnp.logical_and(middle, z + dz == far_dst)
             want = there
@@ -150,32 +158,62 @@
     def send_unit(u, early, late):
         each_near(lambda slot, dz: zr_copy(u, z, dz, slot).start(), early, late)
 
+    def start_q():
+        for cand in range(2):
+            for k in range(NY * NC):
+                q_copy(k, cand).start()
+
+    def unit_of(i):
+        return i - 2 + jnp.where(i - 2 >= y, 1, 0)
+
+    def relay_late(i):
+        u = unit_of(i + AHEAD)
+        send_unit(u, False, True)
+
+    def relay_resp(i):
+        u = unit_of(i)
+
+        @pl.when(middle)
+        def _():
+            landed(rbuf.at[u // NY, lax.rem(u, NY), far_src], zr_r.at[u, far_src])
+            zr_copy(u, far_src, far_dst, 4).start()
+
+        @pl.when(i + AHEAD < UNITS + 1)
+        def _():
+            relay_late(i)
+
+    for j in range(NC):
+        landed(rbuf.at[:, y, z, j], r_r.at[y * NC + j])
+    send_unit(y, True, True)
+    start_q()
     for i in range(NY):
         for j in range(NC):
             landed(pbuf.at[i, z, j], p_r.at[i * NC + j])
     each_near(lambda slot, dz: zp_copy(z, dz, slot).start(), True, True)
     for i in range(NY):
-        for j in range(NC):
-            landed(rbuf.at[:, i, z, j], r_r.at[i * NC + j])
+        @pl.when(i != y)
+        def _(i=i):
+            for j in range(NC):
+                landed(rbuf.at[:, i, z, j], r_r.at[i * NC + j])
     for u in range(UNITS):
-        send_unit(u, True, u < AHEAD)
-
-    def relay_resp(u):
-        @pl.when(middle)
-        def _():
-            landed(rbuf.at[u // NY, u % NY, far_src], zr_r.at[u, far_src])
-            zr_copy(u, far_src, far_dst, 4).start()
-
-        @pl.when(u + AHEAD < UNITS)
-        def _():
-            send_unit(u + AHEAD, False, True)
+        @pl.when(u != y)
+        def _(u=u):
+            send_unit(u, True, False)
+
+    @pl.when(middle)
+    def _():
+        landed(rbuf.at[0, y, far_src], zr_r.at[y, far_src])
+        zr_copy(y, far_src, far_dst, 4).start()
+
+    relay_late(0)
 
     @pl.when(middle)
     def _():
         landed(pbuf.at[:, far_src], zp_r.at[far_src])
         zp_copy(far_src, far_dst, 4).start()
 
-    relay_resp(0)
+    relay_late(1)
+    relay_resp(2)
 
     row_at = lax.broadcasted_iota(jnp.int32, (NC * ROWS, SEG), 0) + z * (NC * ROWS)
     col_at = lax.broadcasted_iota(jnp.int32, (NC * ROWS, SEG), 1)
@@ -205,6 +243,32 @@
     vp[:, :HD] = jnp.where(live, vals, 0.0).astype(jnp.bfloat16)
     vp[:, HD:] = jnp.where(live, 1.0, 0.0).astype(jnp.bfloat16)
 
+    def o_ref(cand, index, t):
+        return out.at[0, cand, :, pl.ds(pl.multiple_of(index * QW + t * TW, TW), TW)]
+
+    def o_remote(u, t, j):
+        cand, g = u // NY, lax.rem(u, NY)
+        return remote(
+            obuf.at[cand, g, t, j], o_ref(cand, mine, t), o_s.at[u, t, j], o_r.at[cand, t, mine],
+            (p, seq_of(g * NC + j, z)),
+        )
+
+    def o_local(u, t, j):
+        cand, g = u // NY, lax.rem(u, NY)
+        return pltpu.make_async_copy(obuf.at[cand, g, t, j], o_ref(cand, mine, t), o_r.at[cand, t, mine])
+
+    def send_out(u, t):
+        for j in range(NC):
+            to = lax.rem(u, NY) * NC + j
+
+            @pl.when(to == mine)
+            def _(j=j):
+                o_local(u, t, j).start()
+
+            @pl.when(to != mine)
+            def _(j=j):
+                o_remote(u, t, j).start()
+
     dims = (((1,), (1,)), ((), ()))
 
     def lane_max(x):
@@ -213,104 +277,82 @@
             best = jnp.maximum(best, x[:, t * HD : (t + 1) * HD])
         return best
 
-    def attend(u):
-        cand, g = u // NY, lax.rem(u, NY)
-
-        def q_rows():
-            block = qbuf[cand, g]
-            return jnp.concatenate(
-                [block[:, :, h * HD : (h + 1) * HD].reshape(NC * ROWS, HD) for h in range(GROUP)], axis=0
+    def attend(u, g):
+        cand = u // NY
+        block = qbuf.at[cand, g]
+        segments = [None] + list(range(g + 1))
+
+        def span(seg):
+            return (0, NPROMPT) if seg is None else (NPROMPT + seg * SEG, SEG)
+
+        def rows_of(t):
+            return pl.ds(t * TR, TR)
+
+        def resp_rows(seg):
+            return rbuf[cand, seg].reshape(SEG, KVW)
+
+        def score(t, seg):
+            q = block[:, :, t * TW : (t + 1) * TW]
+            q = jnp.concatenate(
+                [q[:, :, h * HD : (h + 1) * HD].reshape(NC * ROWS, HD) for h in range(TILE)], axis=0
             )
-
-        mbuf[...] = jnp.full((RT, HD), NEG, jnp.float32)
-
-        def score_prompt(t, _):
-            at = pl.multiple_of(t * PCH, PCH)
-            sc = lax.dot_general(q_rows(), kp[pl.ds(at, PCH), :], dims, preferred_element_type=jnp.float32)
-            sbuf[:, pl.ds(at, PCH)] = sc
-            mbuf[...] = jnp.maximum(mbuf[...], lane_max(sc))
-            return 0
-
-        lax.fori_loop(0, NPROMPT // PCH, score_prompt, 0)
-
-        def resp_keys(t):
-            return rbuf[cand, t].reshape(SEG, KVW)
-
-        def score_resp(t, _):
-            at = pl.multiple_of(NPROMPT + t * SEG, HD)
-            sc = lax.dot_general(q_rows(), resp_keys(t)[:, :HD], dims, preferred_element_type=jnp.float32)
-            sbuf[:, pl.ds(at, SEG)] = sc
-            mbuf[...] = jnp.maximum(mbuf[...], lane_max(sc))
-            return 0
-
-        lax.fori_loop(0, g, score_resp, 0)
-        at = pl.multiple_of(NPROMPT + g * SEG, HD)
-        sc = lax.dot_general(q_rows(), resp_keys(g)[:, :HD], dims, preferred_element_type=jnp.float32)
-        sc = (sc.reshape(GROUP, NC * ROWS, SEG) + bias[...][None]).reshape(RT, SEG)
-        sbuf[:, pl.ds(at, SEG)] = sc
-        best = jnp.max(jnp.maximum(mbuf[...], lane_max(sc)), axis=1, keepdims=True) * SCALE
-        mbuf[...] = jnp.broadcast_to(best, (RT, HD))
-        accbuf[...] = jnp.zeros((RT, KVW), jnp.float32)
-
-        @pl.when(u < UNITS - 1)
+            at, size = span(seg)
+            k = kp[...] if seg is None else resp_rows(seg)[:, :HD]
+            sc = lax.dot_general(q, k, dims, preferred_element_type=jnp.float32)
+            if seg == g:
+                sc = (sc.reshape(TILE, NC * ROWS, SEG) + bias[...][None]).reshape(TR, SEG)
+            sbuf[rows_of(t), pl.ds(at, size)] = sc
+            best = lane_max(sc)
+            if seg is not None:
+                best = jnp.maximum(mbuf[rows_of(t)], best)
+            if seg == g:
+                best = jnp.broadcast_to(jnp.max(best, axis=1, keepdims=True) * SCALE, (TR, HD))
+            mbuf[rows_of(t)] = best
+
+        def add(t, seg):
+            at, size = span(seg)
+            m = jnp.concatenate([mbuf[rows_of(t)]] * (size // HD), axis=1)
+            w = jnp.exp2(sbuf[rows_of(t), pl.ds(at, size)] * SCALE - m).astype(jnp.bfloat16)
+            if seg is None:
+                v = vp[...]
+            else:
+                v = jnp.concatenate([resp_rows(seg)[:, HD:], jnp.ones((SEG, HD), jnp.bfloat16)], axis=1)
+            part = jnp.dot(w, v, preferred_element_type=jnp.float32)
+            accbuf[rows_of(t)] = part if seg is None else accbuf[rows_of(t)] + part
+
+        def finish(t):
+            acc = accbuf[rows_of(t)]
+            res = (acc[:, :HD] / acc[:, HD:]).reshape(TILE, NC * ROWS, HD)
+            pos = lax.broadcasted_iota(jnp.int32, (NC * ROWS, HD), 0) + (g * SEG + z * (NC * ROWS))
+            alive = pos < rlen[0, cand]
+            for h in range(TILE):
+                piece = jnp.where(alive, res[h], 0.0).astype(jnp.bfloat16)
+                obuf[cand, g, t, :, :, h * HD : (h + 1) * HD] = piece.reshape(NC, ROWS, HD)
+            send_out(u, t)
+
+        for seg in segments:
+            score(0, seg)
+
+        @pl.when(u + 3 < UNITS + 1)
         def _():
-            relay_resp(u + 1)
-
-        def weights(at, size):
-            m = mbuf[...]
-            m = jnp.concatenate([m] * (size // HD), axis=1)
-            return jnp.exp2(sbuf[:, pl.ds(at, size)] * SCALE - m).astype(jnp.bfloat16)
-
-        def add_prompt(t, _):
-            at = pl.multiple_of(t * PCH, PCH)
-            accbuf[...] += jnp.dot(weights(at, PCH), vp[pl.ds(at, PCH), :], preferred_element_type=jnp.float32)
-            return 0
-
-        lax.fori_loop(0, NPROMPT // PCH, add_prompt, 0)
-
-        def add_resp(t, _):
-            at = pl.multiple_of(NPROMPT + t * SEG, HD)
-            vx = jnp.concatenate([resp_keys(t)[:, HD:], jnp.ones((SEG, HD), jnp.bfloat16)], axis=1)
-            accbuf[...] += jnp.dot(weights(at, SEG), vx, preferred_element_type=jnp.float32)
-            return 0
-
-        lax.fori_loop(0, g + 1, add_resp, 0)
-        acc = accbuf[...]
-        res = (acc[:, :HD] / acc[:, HD:]).reshape(GROUP, NC * ROWS, HD)
-        pos = lax.broadcasted_iota(jnp.int32, (NC * ROWS, HD), 0) + (g * SEG + z * (NC * ROWS))
-        alive = pos < rlen[0, cand]
-        for h in range(GROUP):
-            piece = jnp.where(alive, res[h], 0.0).astype(jnp.bfloat16)
-            obuf[cand, g, :, :, h * HD : (h + 1) * HD] = piece.reshape(NC, ROWS, HD)
-
-    def o_ref(cand, index):
-        return out.at[0, cand, :, pl.ds(pl.multiple_of(index * QW, QW), QW)]
-
-    def o_remote(u, j):
-        cand, g = u // NY, lax.rem(u, NY)
-        return remote(
-            obuf.at[cand, g, j], o_ref(cand, mine), o_s.at[u, j], o_r.at[cand, mine],
-            (p, seq_of(g * NC + j, z)),
-        )
-
-    def o_local(u, j):
-        cand, g = u // NY, lax.rem(u, NY)
-        return pltpu.make_async_copy(obuf.at[cand, g, j], o_ref(cand, mine), o_r.at[cand, mine])
+            relay_resp(u + 3)
+
+        for t in range(TILES):
+            for seg in segments:
+                if t + 1 < TILES:
+                    score(t + 1, seg)
+                add(t, seg)
+            finish(t)
 
     def unit_step(u, _):
         cand, g = u // NY, lax.rem(u, NY)
         for j in range(NC):
             landed(qbuf.at[cand, g, j], q_r.at[cand, g * NC + j])
         wait_z(lambda zz: rbuf.at[cand, g, zz], lambda zz: zr_r.at[u, zz])
-        attend(u)
-        for j in range(NC):
-            @pl.when(g * NC + j == mine)
-            def _():
-                o_local(u, j).start()
-
-            @pl.when(g * NC + j != mine)
-            def _():
-                o_remote(u, j).start()
+        for k in range(NY):
+            @pl.when(g == k)
+            def _(k=k):
+                attend(u, k)
         return 0
 
     lax.fori_loop(0, UNITS, unit_step, 0)
@@ -338,17 +380,19 @@
         def _():
             zr_copy(u, far_src, far_dst, 4).wait_send()
 
-        for j in range(NC):
-            @pl.when(lax.rem(u, NY) * NC + j != mine)
-            def _():
-                o_remote(u, j).wait_send()
+        for t in range(TILES):
+            for j in range(NC):
+                @pl.when(lax.rem(u, NY) * NC + j != mine)
+                def _(t=t, j=j):
+                    o_remote(u, t, j).wait_send()
         return 0
 
     lax.fori_loop(0, UNITS, end_step, 0)
 
     for cand in range(2):
-        for k in range(NY * NC):
-            landed(o_ref(cand, k), o_r.at[cand, k])
+        for t in range(TILES):
+            for k in range(NY * NC):
+                landed(o_ref(cand, k, t), o_r.at[cand, t, k])
 
 
 def shards(queries, resp_kv, prompt_kv, block_order, prompt_len, resp_len):
@@ -365,7 +409,7 @@
             pltpu.VMEM((2, NY, NC, ROWS, QW), bf16),
             pltpu.VMEM((2, NY, NZ, NC, ROWS, KVW), bf16),
             pltpu.VMEM((NY, NZ, NC, CP, KVW), bf16),
-            pltpu.VMEM((2, NY, NC, ROWS, QW), bf16),
+            pltpu.VMEM((2, NY, TILES, NC, ROWS, TW), bf16),
             pltpu.VMEM((NPROMPT, HD), bf16),
             pltpu.VMEM((NPROMPT, KVW), bf16),
             pltpu.VMEM((RT, NPROMPT + NY * SEG), f32),
@@ -377,7 +421,7 @@
             dma((NP,)), dma((NY * NC,)),
             dma((5,)), dma((NZ,)),
             dma((UNITS, 5)), dma((UNITS, NZ)),
-            dma((UNITS, NC)), dma((2, NY * NC)),
+            dma((UNITS, TILES, NC)), dma((2, TILES, NY * NC)),
         ],
         compiler_params=pltpu.CompilerParams(
             collective_id=0, has_side_effects=True, vmem_limit_bytes=62 * 1024 * 1024

time: 78.1 us -> 73.5 us (0.941)
  Pallas kernels: 74.6 us -> 69.8 us
    pallas_call x1, Pallas kernels: 74.6 us -> 69.8 us  [shards(): pl.pallas_call(kernel, out_shape=jax.ShapeDtypeStruct(queries.shape, bf16...]
where the time goes in v3:
time: 73.5 us; the launch traced here: 73.2 us
  Pallas kernels  69.8 us (95%)
  local copies, waits for them, and re-layouts  2.65 us (4%)
    pallas_call x1, Pallas kernels, shards(): pl.pallas_call(kernel, out_shape=jax.ShapeDtypeStruct(queries.shape, bf16...  69.8 us
    unnamed x1, local copies, waits for them, and re-layouts  2.65 us

profile of v3, /device:TPU:25, one launch (start us, length us, event | category | flops | bytes accessed | tf_op | source)
XLA Modules:
  0.0 73.2 jit_solution(1197089840026494451)
XLA Ops:
  0.7 69.8 %attend.1 = bf16[1,2,48,8192]{3,2,1,0:T(8,128)(2,1)} custom-call(bf16[1,2,48,8192]{3,2,1,0:T(8,128)(2,1)} %q_in.1, bf16[1,2,48,2048]{3,2,1,0:T(8,128)(2,1)} %r_in.1, bf16[8,32,256]{2,1,0:T(8,128)(2,1)} %p_in.1, s32[1,32]{1,0:T(1,128)} %order.1, s32[1]{0:T(128)S(6)} %copy.8.plen, s32[1,2]{1,0:T(1,128)} %rlen.1), custom_call_target="tpu_custom_call" | custom-call | tf_op jit(solution)/shard_map/attend/pallas_call | solution.py:403
  70.5 2.7 %copy.9 = bf16[1,2,48,8192]{3,2,1,0:T(8,128)(2,1)} copy(bf16[1,2,48,8192]{3,2,1,0:T(8,128)(2,1)} %attend.1) | data formatting | bytes 3145728

commit v4 on v3

--- a/solution.py
+++ b/solution.py
@@ -30,6 +30,7 @@
 TW = TILE * HD
 TR = TILE * NC * ROWS
 AHEAD = 2
+EARLY = 1
 
 
 def kernel(
@@ -78,33 +79,41 @@
         greet((p, home))
         greet((mine, s))
 
-    extra = jnp.where(p != mine, 2, 0)
-    pl.semaphore_wait(barrier, (NY * NC - 1) * 2 + (NZ - 1) + (NP - 1) + extra)
 
     def r_copy(k):
         t = at_rel(k)
         src = r_in.at[0, :, :, pl.ds(pl.multiple_of(t * KVW, KVW), KVW)]
         dst = rbuf.at[:, y, z, c]
         if k == 0:
-            return pltpu.make_async_copy(src, dst, r_r.at[mine])
-        return remote(src, dst, r_s.at[k], r_r.at[mine], (p, seq_of(t, z)))
+            return pltpu.make_async_copy(src, dst, r_r.at[y])
+        return remote(src, dst, r_s.at[0], r_r.at[y], (p, seq_of(t, z)))
 
     def q_copy(k, cand):
         t = at_rel(k)
         src = q_in.at[0, cand, :, pl.ds(pl.multiple_of(t * QW, QW), QW)]
-        dst = qbuf.at[cand, y, c]
+        dst = qbuf.at[cand, mine]
         if k == 0:
-            return pltpu.make_async_copy(src, dst, q_r.at[cand, mine])
-        return remote(src, dst, q_s.at[cand, k], q_r.at[cand, mine], (p, seq_of(t, z)))
+            return pltpu.make_async_copy(src, dst, q_r.at[cand, y])
+        return remote(src, dst, q_s.at[0], q_r.at[cand, y], (p, seq_of(t, z)))
 
     def p_copy(k):
         t = lax.rem(p + k, NP)
-        return remote(p_in.at[t], pbuf.at[y, z, c], p_s.at[k], p_r.at[mine], (t, home))
+        return remote(p_in.at[t], pbuf.at[y, z, c], p_s.at[0], p_r.at[0], (t, home))
 
     def p_local():
-        return pltpu.make_async_copy(p_in.at[p], pbuf.at[y, z, c], p_r.at[mine])
+        return pltpu.make_async_copy(p_in.at[p], pbuf.at[y, z, c], p_r.at[0])
 
     r_copy(0).start()
+    for cand in range(2):
+        q_copy(0, cand).start()
+
+    row_at = lax.broadcasted_iota(jnp.int32, (NC * ROWS, SEG), 0) + z * (NC * ROWS)
+    col_at = lax.broadcasted_iota(jnp.int32, (NC * ROWS, SEG), 1)
+    bias[...] = jnp.where(col_at <= row_at, 0.0, NEG)
+
+    extra = jnp.where(p != mine, 2, 0)
+    pl.semaphore_wait(barrier, (NY * NC - 1) * 2 + (NZ - 1) + (NP - 1) + extra)
+
     for k in (1, NY * NC - 1):
         @pl.when(at_rel(k) // NC == y)
         def _(k=k):
@@ -129,20 +138,20 @@
     def z_dev(zz):
         return (p, y * (NZ * NC) + zz * NC + c)
 
-    def zp_copy(src_z, dst_z, slot):
+    def zp_copy(src_z, dst_z):
         ref = pbuf.at[:, src_z]
-        return remote(ref, ref, zp_s.at[slot], zp_r.at[src_z], z_dev(dst_z))
-
-    def zr_copy(u, src_z, dst_z, slot):
+        return remote(ref, ref, zp_s.at[0], zp_r.at[src_z], z_dev(dst_z))
+
+    def zr_copy(u, src_z, dst_z):
         ref = rbuf.at[u // NY, lax.rem(u, NY), src_z]
-        return remote(ref, ref, zr_s.at[u, slot], zr_r.at[u, src_z], z_dev(dst_z))
+        return remote(ref, ref, zr_s.at[0], zr_r.at[u, src_z], z_dev(dst_z))
 
     middle = jnp.logical_and(z > 0, z < NZ - 1)
     far_dst = (z - 1) * (NZ - 1)
     far_src = (NZ - 1) - far_dst
 
     def each_near(act, early, late):
-        for slot, dz in enumerate((2, -2, 1, -1)):
+        for dz in (2, -2, 1, -1):
             there = jnp.logical_and(z + dz >= 0, z + dz < NZ)
             held = jnp.logical_and(middle, z + dz == far_dst)
             want = there
@@ -152,23 +161,22 @@
                 want = jnp.logical_and(there, jnp.logical_not(held))
 
             @pl.when(want)
-            def _(slot=slot, dz=dz):
-                act(slot, z + dz)
+            def _(dz=dz):
+                act(z + dz)
 
     def send_unit(u, early, late):
-        each_near(lambda slot, dz: zr_copy(u, z, dz, slot).start(), early, late)
+        each_near(lambda zz: zr_copy(u, z, zz).start(), early, late)
 
     def start_q():
         for cand in range(2):
-            for k in range(NY * NC):
+            for k in range(1, NY * NC):
                 q_copy(k, cand).start()
 
     def unit_of(i):
         return i - 2 + jnp.where(i - 2 >= y, 1, 0)
 
     def relay_late(i):
-        u = unit_of(i + AHEAD)
-        send_unit(u, False, True)
+        send_unit(unit_of(i + AHEAD), False, True)
 
     def relay_resp(i):
         u = unit_of(i)
@@ -176,48 +184,45 @@
         @pl.when(middle)
         def _():
             landed(rbuf.at[u // NY, lax.rem(u, NY), far_src], zr_r.at[u, far_src])
-            zr_copy(u, far_src, far_dst, 4).start()
+            zr_copy(u, far_src, far_dst).start()
 
         @pl.when(i + AHEAD < UNITS + 1)
         def _():
             relay_late(i)
 
-    for j in range(NC):
-        landed(rbuf.at[:, y, z, j], r_r.at[y * NC + j])
+    landed(rbuf.at[:, y, z], r_r.at[y])
     send_unit(y, True, True)
     start_q()
-    for i in range(NY):
-        for j in range(NC):
-            landed(pbuf.at[i, z, j], p_r.at[i * NC + j])
-    each_near(lambda slot, dz: zp_copy(z, dz, slot).start(), True, True)
+    landed(pbuf.at[:, z], p_r.at[0])
+    each_near(lambda zz: zp_copy(z, zz).start(), True, True)
     for i in range(NY):
         @pl.when(i != y)
         def _(i=i):
-            for j in range(NC):
-                landed(rbuf.at[:, i, z, j], r_r.at[i * NC + j])
+            landed(rbuf.at[:, i, z], r_r.at[i])
     for u in range(UNITS):
         @pl.when(u != y)
         def _(u=u):
             send_unit(u, True, False)
 
+    for i in range(2, AHEAD):
+        send_unit(unit_of(i), False, True)
+
     @pl.when(middle)
     def _():
         landed(rbuf.at[0, y, far_src], zr_r.at[y, far_src])
-        zr_copy(y, far_src, far_dst, 4).start()
+        zr_copy(y, far_src, far_dst).start()
 
     relay_late(0)
 
     @pl.when(middle)
     def _():
         landed(pbuf.at[:, far_src], zp_r.at[far_src])
-        zp_copy(far_src, far_dst, 4).start()
+        zp_copy(far_src, far_dst).start()
 
     relay_late(1)
-    relay_resp(2)
-
-    row_at = lax.broadcasted_iota(jnp.int32, (NC * ROWS, SEG), 0) + z * (NC * ROWS)
-    col_at = lax.broadcasted_iota(jnp.int32, (NC * ROWS, SEG), 1)
-    bias[...] = jnp.where(col_at <= row_at, 0.0, NEG)
+
+    for i in range(2, 3 + EARLY):
+        relay_resp(i)
 
     def wait_z(ref_of, sem_of):
         for k in range(1, NZ):
@@ -249,13 +254,13 @@
     def o_remote(u, t, j):
         cand, g = u // NY, lax.rem(u, NY)
         return remote(
-            obuf.at[cand, g, t, j], o_ref(cand, mine, t), o_s.at[u, t, j], o_r.at[cand, t, mine],
+            obuf.at[cand, t, g * NC + j], o_ref(cand, mine, t), o_s.at[0], o_r.at[0],
             (p, seq_of(g * NC + j, z)),
         )
 
     def o_local(u, t, j):
         cand, g = u // NY, lax.rem(u, NY)
-        return pltpu.make_async_copy(obuf.at[cand, g, t, j], o_ref(cand, mine, t), o_r.at[cand, t, mine])
+        return pltpu.make_async_copy(obuf.at[cand, t, g * NC + j], o_ref(cand, mine, t), o_r.at[0])
 
     def send_out(u, t):
         for j in range(NC):
@@ -279,7 +284,7 @@
 
     def attend(u, g):
         cand = u // NY
-        block = qbuf.at[cand, g]
+        block = qbuf.at[cand, pl.ds(g * NC, NC)]
         segments = [None] + list(range(g + 1))
 
         def span(seg):
@@ -327,15 +332,14 @@
             alive = pos < rlen[0, cand]
             for h in range(TILE):
                 piece = jnp.where(alive, res[h], 0.0).astype(jnp.bfloat16)
-                obuf[cand, g, t, :, :, h * HD : (h + 1) * HD] = piece.reshape(NC, ROWS, HD)
+                obuf[cand, t, g * NC : (g + 1) * NC, :, h * HD : (h + 1) * HD] = piece.reshape(NC, ROWS, HD)
             send_out(u, t)
 
-        for seg in segments:
+        for seg in segments[:-1]:
             score(0, seg)
 
-        @pl.when(u + 3 < UNITS + 1)
-        def _():
-            relay_resp(u + 3)
+        wait_z(lambda zz: rbuf.at[cand, g, zz], lambda zz: zr_r.at[u, zz])
+        score(0, g)
 
         for t in range(TILES):
             for seg in segments:
@@ -346,9 +350,11 @@
 
     def unit_step(u, _):
         cand, g = u // NY, lax.rem(u, NY)
-        for j in range(NC):
-            landed(qbuf.at[cand, g, j], q_r.at[cand, g * NC + j])
-        wait_z(lambda zz: rbuf.at[cand, g, zz], lambda zz: zr_r.at[u, zz])
+        @pl.when(u + 3 + EARLY < UNITS + 1)
+        def _():
+            relay_resp(u + 3 + EARLY)
+
+        landed(qbuf.at[cand, pl.ds(g * NC, NC)], q_r.at[cand, g])
         for k in range(NY):
             @pl.when(g == k)
             def _(k=k):
@@ -357,42 +363,30 @@
 
     lax.fori_loop(0, UNITS, unit_step, 0)
 
-    for k in range(1, NY * NC):
-        for cand in range(2):
-            q_copy(k, cand).wait_send()
-        r_copy(k).wait_send()
-        p_copy(k).wait_send()
+    most = NY * NC - 1
+    landed(qbuf.at[:, pl.ds(0, most)], q_s.at[0])
+    landed(r_in.at[0, :, :, pl.ds(0, most * KVW)], r_s.at[0])
 
     @pl.when(p != mine)
     def _():
-        p_copy(0).wait_send()
-
-    each_near(lambda slot, dz: zp_copy(z, dz, slot).wait_send(), True, True)
+        landed(p_in, p_s.at[0])
+
+    @pl.when(p == mine)
+    def _():
+        landed(p_in.at[pl.ds(0, NP - 1)], p_s.at[0])
 
     @pl.when(middle)
     def _():
-        zp_copy(far_src, far_dst, 4).wait_send()
-
-    def end_step(u, _):
-        each_near(lambda slot, dz: zr_copy(u, z, dz, slot).wait_send(), True, True)
-
-        @pl.when(middle)
-        def _():
-            zr_copy(u, far_src, far_dst, 4).wait_send()
-
-        for t in range(TILES):
-            for j in range(NC):
-                @pl.when(lax.rem(u, NY) * NC + j != mine)
-                def _(t=t, j=j):
-                    o_remote(u, t, j).wait_send()
-        return 0
-
-    lax.fori_loop(0, UNITS, end_step, 0)
-
-    for cand in range(2):
-        for t in range(TILES):
-            for k in range(NY * NC):
-                landed(o_ref(cand, k, t), o_r.at[cand, t, k])
+        landed(pbuf, zp_s.at[0])
+        landed(rbuf, zr_s.at[0])
+
+    @pl.when(jnp.logical_not(middle))
+    def _():
+        landed(pbuf.at[:, pl.ds(0, 2)], zp_s.at[0])
+        landed(rbuf.at[:, :, pl.ds(0, 2)], zr_s.at[0])
+
+    landed(obuf.at[:, :, pl.ds(0, most)], o_s.at[0])
+    landed(out, o_r.at[0])
 
 
 def shards(queries, resp_kv, prompt_kv, block_order, prompt_len, resp_len):
@@ -406,22 +400,22 @@
         in_specs=[any_spec] * 3 + [smem] * 3,
         out_specs=any_spec,
         scratch_shapes=[
-            pltpu.VMEM((2, NY, NC, ROWS, QW), bf16),
+            pltpu.VMEM((2, NY * NC, ROWS, QW), bf16),
             pltpu.VMEM((2, NY, NZ, NC, ROWS, KVW), bf16),
             pltpu.VMEM((NY, NZ, NC, CP, KVW), bf16),
-            pltpu.VMEM((2, NY, TILES, NC, ROWS, TW), bf16),
+            pltpu.VMEM((2, TILES, NY * NC, ROWS, TW), bf16),
             pltpu.VMEM((NPROMPT, HD), bf16),
             pltpu.VMEM((NPROMPT, KVW), bf16),
             pltpu.VMEM((RT, NPROMPT + NY * SEG), f32),
             pltpu.VMEM((RT, HD), f32),
             pltpu.VMEM((RT, KVW), f32),
             pltpu.VMEM((NC * ROWS, SEG), f32),
-            dma((2, NY * NC)), dma((2, NY * NC)),
-            dma((NY * NC,)), dma((NY * NC,)),
-            dma((NP,)), dma((NY * NC,)),
-            dma((5,)), dma((NZ,)),
-            dma((UNITS, 5)), dma((UNITS, NZ)),
-            dma((UNITS, TILES, NC)), dma((2, TILES, NY * NC)),
+            dma((1,)), dma((2, NY)),
+            dma((1,)), dma((NY,)),
+            dma((1,)), dma((1,)),
+            dma((1,)), dma((NZ,)),
+            dma((1,)), dma((UNITS, NZ)),
+            dma((1,)), dma((1,)),
         ],
         compiler_params=pltpu.CompilerParams(
             collective_id=0, has_side_effects=True, vmem_limit_bytes=62 * 1024 * 1024

time: 73.5 us -> 70.4 us (0.958)
  Pallas kernels: 69.8 us -> 66.8 us
    pallas_call x1, Pallas kernels: 69.8 us -> 66.8 us  [shards(): pl.pallas_call(kernel, out_shape=jax.ShapeDtypeStruct(queries.shape, bf16...]
where the time goes in v4:
time: 70.4 us; the launch traced here: 70.1 us
  Pallas kernels  66.8 us (95%)
  local copies, waits for them, and re-layouts  2.65 us (4%)
    pallas_call x1, Pallas kernels, shards(): pl.pallas_call(kernel, out_shape=jax.ShapeDtypeStruct(queries.shape, bf16...  66.8 us
    unnamed x1, local copies, waits for them, and re-layouts  2.65 us

profile of v4, /device:TPU:25, one launch (start us, length us, event | category | flops | bytes accessed | tf_op | source)
XLA Modules:
  0.0 70.1 jit_solution(1526492409145808033)
XLA Ops:
  0.7 66.8 %attend.1 = bf16[1,2,48,8192]{3,2,1,0:T(8,128)(2,1)} custom-call(bf16[1,2,48,8192]{3,2,1,0:T(8,128)(2,1)} %q_in.1, bf16[1,2,48,2048]{3,2,1,0:T(8,128)(2,1)} %r_in.1, bf16[8,32,256]{2,1,0:T(8,128)(2,1)} %p_in.1, s32[1,32]{1,0:T(1,128)} %order.1, s32[1]{0:T(128)S(6)} %copy.8.plen, s32[1,2]{1,0:T(1,128)} %rlen.1), custom_call_target="tpu_custom_call" | custom-call | tf_op jit(solution)/shard_map/attend/pallas_call | solution.py:397
  67.4 2.7 %copy.9 = bf16[1,2,48,8192]{3,2,1,0:T(8,128)(2,1)} copy(bf16[1,2,48,8192]{3,2,1,0:T(8,128)(2,1)} %attend.1) | data formatting | bytes 3145728

commit v5 on v4

--- a/solution.py
+++ b/solution.py
@@ -107,6 +107,11 @@
     for cand in range(2):
         q_copy(0, cand).start()
 
+    for zz in range(1, NZ):
+        @pl.when(zz > z)
+        def _(zz=zz):
+            rbuf[:, NY - 1, zz] = jnp.zeros((2, NC, ROWS, KVW), jnp.bfloat16)
+
     row_at = lax.broadcasted_iota(jnp.int32, (NC * ROWS, SEG), 0) + z * (NC * ROWS)
     col_at = lax.broadcasted_iota(jnp.int32, (NC * ROWS, SEG), 1)
     bias[...] = jnp.where(col_at <= row_at, 0.0, NEG)
@@ -147,12 +152,18 @@
         return remote(ref, ref, zr_s.at[0], zr_r.at[u, src_z], z_dev(dst_z))
 
     middle = jnp.logical_and(z > 0, z < NZ - 1)
+
+    def relays(u):
+        return jnp.logical_and(middle, jnp.logical_or(lax.rem(u, NY) < NY - 1, z == NZ - 2))
+
     far_dst = (z - 1) * (NZ - 1)
     far_src = (NZ - 1) - far_dst
 
-    def each_near(act, early, late):
+    def each_near(act, early, late, last=False):
         for dz in (2, -2, 1, -1):
             there = jnp.logical_and(z + dz >= 0, z + dz < NZ)
+            if dz < 0:
+                there = jnp.logical_and(there, jnp.logical_not(last))
             held = jnp.logical_and(middle, z + dz == far_dst)
             want = there
             if not early:
@@ -165,7 +176,7 @@
                 act(z + dz)
 
     def send_unit(u, early, late):
-        each_near(lambda zz: zr_copy(u, z, zz).start(), early, late)
+        each_near(lambda zz: zr_copy(u, z, zz).start(), early, late, lax.rem(u, NY) == NY - 1)
 
     def start_q():
         for cand in range(2):
@@ -181,7 +192,7 @@
     def relay_resp(i):
         u = unit_of(i)
 
-        @pl.when(middle)
+        @pl.when(relays(u))
         def _():
             landed(rbuf.at[u // NY, lax.rem(u, NY), far_src], zr_r.at[u, far_src])
             zr_copy(u, far_src, far_dst).start()
@@ -207,7 +218,7 @@
     for i in range(2, AHEAD):
         send_unit(unit_of(i), False, True)
 
-    @pl.when(middle)
+    @pl.when(relays(y))
     def _():
         landed(rbuf.at[0, y, far_src], zr_r.at[y, far_src])
         zr_copy(y, far_src, far_dst).start()
@@ -224,12 +235,12 @@
     for i in range(2, 3 + EARLY):
         relay_resp(i)
 
-    def wait_z(ref_of, sem_of):
+    def wait_z(ref_of, sem_of, last=False):
         for k in range(1, NZ):
             src = lax.rem(z + k, NZ)
             relayed = jnp.logical_and(middle, src == far_src)
 
-            @pl.when(jnp.logical_not(relayed))
+            @pl.when(jnp.logical_and(jnp.logical_not(relayed), src < z) if last else jnp.logical_not(relayed))
             def _():
                 landed(ref_of(src), sem_of(src))
 
@@ -338,7 +349,7 @@
         for seg in segments[:-1]:
             score(0, seg)
 
-        wait_z(lambda zz: rbuf.at[cand, g, zz], lambda zz: zr_r.at[u, zz])
+        wait_z(lambda zz: rbuf.at[cand, g, zz], lambda zz: zr_r.at[u, zz], g == NY - 1)
         score(0, g)
 
         for t in range(TILES):
@@ -378,12 +389,19 @@
     @pl.when(middle)
     def _():
         landed(pbuf, zp_s.at[0])
-        landed(rbuf, zr_s.at[0])
+        landed(qbuf.at[:, pl.ds(0, 7)], zr_s.at[0])
 
     @pl.when(jnp.logical_not(middle))
     def _():
         landed(pbuf.at[:, pl.ds(0, 2)], zp_s.at[0])
-        landed(rbuf.at[:, :, pl.ds(0, 2)], zr_s.at[0])
+
+    @pl.when(z == 0)
+    def _():
+        landed(qbuf.at[:, pl.ds(0, 4)], zr_s.at[0])
+
+    @pl.when(z == NZ - 1)
+    def _():
+        landed(qbuf.at[:, pl.ds(0, 3)], zr_s.at[0])
 
     landed(obuf.at[:, :, pl.ds(0, most)], o_s.at[0])
     landed(out, o_r.at[0])

time: 70.4 us -> 69.5 us (0.987)
  Pallas kernels: 66.8 us -> 65.6 us
    pallas_call x1, Pallas kernels: 66.8 us -> 65.6 us  [shards(): pl.pallas_call(kernel, out_shape=jax.ShapeDtypeStruct(queries.shape, bf16...]
where the time goes in v5:
time: 69.5 us; the launch traced here: 69 us
  Pallas kernels  65.6 us (94%)
  local copies, waits for them, and re-layouts  2.65 us (4%)
    pallas_call x1, Pallas kernels, shards(): pl.pallas_call(kernel, out_shape=jax.ShapeDtypeStruct(queries.shape, bf16...  65.6 us
    unnamed x1, local copies, waits for them, and re-layouts  2.65 us

profile of v5, /device:TPU:25, one launch (start us, length us, event | category | flops | bytes accessed | tf_op | source)
XLA Modules:
  0.0 69.0 jit_solution(9945696054661139789)
XLA Ops:
  0.7 65.6 %attend.1 = bf16[1,2,48,8192]{3,2,1,0:T(8,128)(2,1)} custom-call(bf16[1,2,48,8192]{3,2,1,0:T(8,128)(2,1)} %q_in.1, bf16[1,2,48,2048]{3,2,1,0:T(8,128)(2,1)} %r_in.1, bf16[8,32,256]{2,1,0:T(8,128)(2,1)} %p_in.1, s32[1,32]{1,0:T(1,128)} %order.1, s32[1]{0:T(128)S(6)} %copy.8.plen, s32[1,2]{1,0:T(1,128)} %rlen.1), custom_call_target="tpu_custom_call" | custom-call | tf_op jit(solution)/shard_map/attend/pallas_call | solution.py:415
  66.3 2.7 %copy.9 = bf16[1,2,48,8192]{3,2,1,0:T(8,128)(2,1)} copy(bf16[1,2,48,8192]{3,2,1,0:T(8,128)(2,1)} %attend.1) | data formatting | bytes 3145728

commit v6 on v5

--- a/solution.py
+++ b/solution.py
@@ -24,6 +24,7 @@
 SCALE = math.log2(math.e) / math.sqrt(HD)
 MESH = pl.DeviceIdType.MESH
 NEG = -1e30
+TOP = 3.4e38
 UNITS = 2 * NY
 TILE = 4
 TILES = GROUP // TILE
@@ -35,7 +36,7 @@
 
 def kernel(
     q_in, r_in, p_in, order, plen, rlen, out,
-    qbuf, rbuf, pbuf, obuf, kp, vp, sbuf, mbuf, accbuf, bias,
+    qbuf, rbuf, pbuf, obuf, kp, vp, sbuf, mbuf, accbuf, bound,
     q_s, q_r, r_s, r_r, p_s, p_r, zp_s, zp_r, zr_s, zr_r, o_s, o_r,
 ):
     p = lax.axis_index("prompt")
@@ -114,7 +115,7 @@
 
     row_at = lax.broadcasted_iota(jnp.int32, (NC * ROWS, SEG), 0) + z * (NC * ROWS)
     col_at = lax.broadcasted_iota(jnp.int32, (NC * ROWS, SEG), 1)
-    bias[...] = jnp.where(col_at <= row_at, 0.0, NEG)
+    bound[...] = jnp.where(col_at <= row_at, TOP, NEG)
 
     extra = jnp.where(p != mine, 2, 0)
     pl.semaphore_wait(barrier, (NY * NC - 1) * 2 + (NZ - 1) + (NP - 1) + extra)
@@ -316,7 +317,7 @@
             k = kp[...] if seg is None else resp_rows(seg)[:, :HD]
             sc = lax.dot_general(q, k, dims, preferred_element_type=jnp.float32)
             if seg == g:
-                sc = (sc.reshape(TILE, NC * ROWS, SEG) + bias[...][None]).reshape(TR, SEG)
+                sc = jnp.minimum(sc.reshape(TILE, NC * ROWS, SEG), bound[...][None]).reshape(TR, SEG)
             sbuf[rows_of(t), pl.ds(at, size)] = sc
             best = lane_max(sc)
             if seg is not None:

time: 69.5 us -> 69.5 us (level)
  no operation moved by 1% of the time
where the time goes in v6:
time: 69.5 us; the launch traced here: 69 us
  Pallas kernels  65.6 us (94%)
  local copies, waits for them, and re-layouts  2.65 us (4%)
    pallas_call x1, Pallas kernels, shards(): pl.pallas_call(kernel, out_shape=jax.ShapeDtypeStruct(queries.shape, bf16...  65.6 us
    unnamed x1, local copies, waits for them, and re-layouts  2.65 us

profile of v6, /device:TPU:25, one launch (start us, length us, event | category | flops | bytes accessed | tf_op | source)
XLA Modules:
  0.0 69.0 jit_solution(11204624296812315234)
XLA Ops:
  0.7 65.6 %attend.1 = bf16[1,2,48,8192]{3,2,1,0:T(8,128)(2,1)} custom-call(bf16[1,2,48,8192]{3,2,1,0:T(8,128)(2,1)} %q_in.1, bf16[1,2,48,2048]{3,2,1,0:T(8,128)(2,1)} %r_in.1, bf16[8,32,256]{2,1,0:T(8,128)(2,1)} %p_in.1, s32[1,32]{1,0:T(1,128)} %order.1, s32[1]{0:T(128)S(6)} %copy.8.plen, s32[1,2]{1,0:T(1,128)} %rlen.1), custom_call_target="tpu_custom_call" | custom-call | tf_op jit(solution)/shard_map/attend/pallas_call | solution.py:416
  66.3 2.7 %copy.9 = bf16[1,2,48,8192]{3,2,1,0:T(8,128)(2,1)} copy(bf16[1,2,48,8192]{3,2,1,0:T(8,128)(2,1)} %attend.1) | data formatting | bytes 3145728
